TPU v7x, 32 devices: a whole 2x2x4 slice. The times are simulated.
32 devices in a mesh: row: 4 (over y, x), col: 4 (over z), exp: 2 (over core).
Axes of the slice: x: 2, y: 2, z: 4, core: 2. Of those that a mesh axis runs over, the one named last changes fastest.
Arguments:
- hidden_in: bfloat16 [2, 2048, 2048], P('exp', ('row', 'col')), may hold values from -6 to 6
- out_grad: bfloat16 [2, 2048, 2048], P('exp', ('row', 'col')), may hold values from -6 to 6
- attn_gain: bfloat16 [2048], replicated, may hold values from 0.5 to 1.5
- w_qkv: bfloat16 [2048, 6144], P('row', 'col'), may hold values from -0.125 to 0.125
- q_gain: bfloat16 [2048], replicated, may hold values from 0.796875 to 1.796875
- k_gain: bfloat16 [2048], replicated, may hold values from 0.796875 to 1.796875
- w_out: bfloat16 [2048, 2048], P('col', 'row'), may hold values from -0.5 to 0.5
- moe_gain: bfloat16 [2048], replicated, may hold values from 0.5 to 1.5
- router: bfloat16 [2048, 16], replicated, may hold values from -0.0625 to 0.0625
- w_gate: bfloat16 [32, 2048, 512], P(('row', 'col', 'exp')), may hold values from -0.125 to 0.125
- w_up: bfloat16 [32, 2048, 512], P(('row', 'col', 'exp')), may hold values from -0.125 to 0.125
- w_down: bfloat16 [32, 512, 2048], P(('row', 'col', 'exp')), may hold values from -6 to 6
- routes: int32 [2, 2048, 8], P('exp', ('row', 'col')), may hold values from 0 to 15, all different within a row; in each aligned block of 128 rows (0 to 127, 128 to 255, ..., all dimensions but the last counted through in order) at most 128 rows name the same one
- doc_cuts: int32 [1, 2], replicated, may hold values from 1 to 4095, as said below
Outputs:
- out_hidden: bfloat16 [2, 2048, 2048], P('exp', ('row', 'col'))
- grad_hidden: float32 [2, 2048, 2048], P('exp', ('row', 'col'))
- grad_attn_gain: float32 [2048], replicated
- grad_qkv: float32 [2048, 6144], P('row', 'col')
- grad_q_gain: float32 [2048], replicated
- grad_k_gain: float32 [2048], replicated
- grad_w_out: float32 [2048, 2048], P('col', 'row')
- grad_moe_gain: float32 [2048], replicated
- grad_router: float32 [2048, 16], replicated
- grad_gate: float32 [32, 2048, 512], P(('row', 'col', 'exp'))
- grad_up: float32 [32, 2048, 512], P(('row', 'col', 'exp'))
- grad_down: float32 [32, 512, 2048], P(('row', 'col', 'exp'))
Inputs may be any that keep to these rules, and one draw needn't show every extreme that they name: `routes`: each token names 8 different experts. In each aligned block of 128 tokens (the tokens of one device) no expert is named by more than 128 tokens, a bound that some block reaches. A sequence's documents are its tokens before doc_cuts[s, 0], those from doc_cuts[s, 0] up to doc_cuts[s, 1], and the rest; doc_cuts[s, 0] is at most 64 and doc_cuts[s, 1] at least 4032.
All inputs are finite; a program needn't handle non-finite values.
Results may differ from a plain program's by a relative error of at most 0.024.
Values may be sent and summed in bfloat16 or wider, within the bound.
A program may use at most 320 MiB of HBM per device.

v0:
```python
import functools
import math

import jax
import jax.numpy as jnp
from jax import lax
from jax.experimental import pallas as pl
from jax.experimental.pallas import tpu as pltpu
from jax.sharding import PartitionSpec as P

HD = 128
EPSILON = 1e-05
ROPE_BASE = 10000.0
MASKED = -1e30
BF16 = jnp.bfloat16
F32 = jnp.float32


def matmul(left, right):
    return jnp.dot(left, right, preferred_element_type=F32)


def contract_rows(left, right):
    return lax.dot_general(left, right, (((0,), (0,)), ((), ())), preferred_element_type=F32)


def contract_cols(left, right):
    return lax.dot_general(left, right, (((1,), (1,)), ((), ())), preferred_element_type=F32)


def rms_scale(values):
    return lax.rsqrt(jnp.mean(values * values, axis=-1, keepdims=True) + EPSILON)


def rope_tables(position, width):
    frequency = ROPE_BASE ** (-jnp.arange(0, width, 2, dtype=F32) / width)
    angle = position.astype(F32)[:, None] * frequency[None, :]
    return (
        jnp.concatenate([jnp.cos(angle)] * 2, axis=-1),
        jnp.concatenate([jnp.sin(angle)] * 2, axis=-1),
    )


def rotate(values, cosine, sine):
    half = values.shape[-1] // 2
    turned = jnp.concatenate([-values[..., half:], values[..., :half]], axis=-1)
    return values * cosine + turned * sine


def rotate_back(values, cosine, sine):
    half = values.shape[-1] // 2
    turned = values * sine
    return values * cosine + jnp.concatenate([turned[..., half:], -turned[..., :half]], axis=-1)


def doc_positions(places, cuts):
    first = (places >= cuts[0]).astype(jnp.int32)
    second = (places >= cuts[1]).astype(jnp.int32)
    start = first * cuts[0] + second * (cuts[1] - cuts[0])
    return (first + second, places - start)


def from_behind(value, axis, steps):
    count = lax.axis_size(axis)
    initial, last = (max(0, -steps), min(count, count - steps))
    return lax.ppermute(value, axis, [(source, source + steps) for source in range(initial, last)])


def rows_to_heads(values):
    count = lax.axis_size("row")
    rows, heads, width = values.shape
    moved = lax.all_to_all(values.transpose(1, 0, 2), "row", split_axis=0, concat_axis=0, tiled=True)
    return moved.reshape(count * rows, width)


def heads_to_rows(values):
    count = lax.axis_size("row")
    rows, width = values.shape
    moved = lax.all_to_all(
        values.reshape(count, rows // count, width), "row", split_axis=0, concat_axis=0, tiled=True
    )
    return moved.transpose(1, 0, 2)


def heads_to_tokens(values):
    row_count, col_count = lax.axis_size("row"), lax.axis_size("col")
    rows = values.shape[0] // (row_count * col_count)
    moved = lax.all_to_all(
        values.reshape(row_count * col_count, rows, HD),
        ("row", "col"),
        split_axis=0,
        concat_axis=0,
        tiled=True,
    )
    moved = moved.reshape(row_count, col_count, rows, HD).transpose(2, 1, 0, 3)
    return moved.reshape(rows, row_count * col_count * HD)


def tokens_to_heads(values):
    row_count, col_count = lax.axis_size("row"), lax.axis_size("col")
    rows = values.shape[0]
    parted = values.reshape(rows, col_count, row_count, HD).transpose(2, 1, 0, 3)
    moved = lax.all_to_all(
        parted.reshape(row_count * col_count, rows, HD),
        ("row", "col"),
        split_axis=0,
        concat_axis=0,
        tiled=True,
    )
    return moved.reshape(row_count * col_count * rows, HD)


MESH = pl.DeviceIdType.MESH
ALL = ("row", "col", "exp")


class Here:
    def __init__(self):
        self.row, self.col, self.core = (lax.axis_index(axis) for axis in ALL)
        self.across = self.row + 1 - 2 * (self.row % 2)
        self.along = (self.row + 2) % 4
        self.opposite = 3 - self.row
        self.rows = (self.row, self.across, self.along, self.opposite)
        half = self.col // 2
        self.near_first = [
            self.col,
            1 + self.col % 2,
            2 - self.col - self.col % 2 + 3 * half,
            3 - 3 * half,
        ]

    def at_row(self, row):
        return (row, self.col, self.core)

    def at_col(self, col):
        return (self.row, col, self.core)

    def other_core(self):
        return (self.row, self.col, 1 - self.core)

    def line_peers(self):
        return [self.at_col((self.col + step) % 4) for step in (1, 2, 3)]

    def group_peers(self):
        steps = range(1, 16)
        return [((self.row + s // 4) % 4, (self.col + s) % 4, self.core) for s in steps]

    def plane_peers(self):
        return [self.at_row(row) for row in self.rows[1:]]


def greet(peers):
    barrier = pltpu.get_barrier_semaphore()
    for peer in peers:
        pl.semaphore_signal(barrier, inc=1, device_id=peer, device_id_type=MESH)
    pl.semaphore_wait(barrier, len(peers))


def greet_near(here):
    barrier = pltpu.get_barrier_semaphore()
    col = here.col

    def signal(peer):
        pl.semaphore_signal(barrier, inc=1, device_id=peer, device_id_type=MESH)

    for peer in (here.other_core(), here.at_row(here.across), here.at_row(here.along)):
        signal(peer)

    @pl.when(col > 0)
    def _():
        signal(here.at_col(col - 1))

    @pl.when(col < 3)
    def _():
        signal(here.at_col(col + 1))

    pl.semaphore_wait(barrier, 3 + (col + 3) // 4 + (6 - col) // 4)


def remote(source, target, send, recv, device):
    return pltpu.make_async_remote_copy(
        src_ref=source,
        dst_ref=target,
        send_sem=send,
        recv_sem=recv,
        device_id=device,
        device_id_type=MESH,
    )


def arrived(target, recv):
    pltpu.make_async_copy(target, target, recv).wait()


def add_into(target, *terms):
    step = 16

    @pl.loop(0, target.shape[0] // step)
    def _(index):
        part = pl.ds(pl.multiple_of(index * step, step), step)
        value = target[part].astype(F32)
        for term in terms:
            value = value + term[part].astype(F32)
        target[part] = value.astype(target.dtype)


SPREAD_SEMS = [pltpu.SemaphoreType.DMA((4,))] * 11 + [pltpu.SemaphoreType.DMA((4, 4))] * 2


class Spread:
    def __init__(self, here, own, block, rows, sems, line=True, plane=True, core=True):
        self.here, self.own, self.block = here, own, block
        self.line, self.plane, self.core = line, plane, core
        (
            self.up_send, self.down_send, self.line_recv,
            self.across_send, self.across_recv, self.along_send, self.along_recv,
            self.one_send, self.one_recv, self.two_send, self.two_recv,
            self.core_send, self.core_recv,
        ) = sems
        self.first, self.second = pl.ds(0, rows // 2), pl.ds(rows // 2, rows // 2)
        self.order = here.near_first if line else [0]
        self.steps = len(self.order)

    def held(self, step):
        here = self.here
        return self.own if step == 0 else self.block(here.row, self.order[step], here.core)

    def up(self, step):
        here, place = self.here, self.order[step]
        target = self.block(here.row, place, here.core)
        recv = self.line_recv.at[place]
        return remote(self.held(step), target, self.up_send.at[place], recv, here.at_col(here.col + 1))

    def down(self, step):
        here, place = self.here, self.order[step]
        target = self.block(here.row, place, here.core)
        recv = self.line_recv.at[place]
        return remote(self.held(step), target, self.down_send.at[place], recv, here.at_col(here.col - 1))

    def to_across(self, step):
        here, place = self.here, self.order[step]
        target = self.block(here.row, place, here.core)
        sems = self.across_send.at[place], self.across_recv.at[place]
        return remote(self.held(step), target, *sems, here.at_row(here.across))

    def to_along(self, step):
        here, place = self.here, self.order[step]
        target = self.block(here.row, place, here.core)
        sems = self.along_send.at[place], self.along_recv.at[place]
        return remote(self.held(step), target, *sems, here.at_row(here.along))

    def corner_one(self, step):
        here, place = self.here, self.order[step]
        part = self.block(here.across, place, here.core).at[self.first]
        sems = self.one_send.at[place], self.one_recv.at[place]
        return remote(part, part, *sems, here.at_row(here.along))

    def corner_two(self, step):
        here, place = self.here, self.order[step]
        part = self.block(here.along, place, here.core).at[self.second]
        sems = self.two_send.at[place], self.two_recv.at[place]
        return remote(part, part, *sems, here.at_row(here.across))

    def to_core(self, which, step):
        here, place = self.here, self.order[step]
        target = self.block(here.rows[which], place, here.core)
        source = self.held(step) if which == 0 else target
        sems = self.core_send.at[which, place], self.core_recv.at[which, place]
        return remote(source, target, *sems, here.other_core())

    def line_step(self, step):
        here, place = self.here, self.order[step]
        if step > 0:
            arrived(self.held(step), self.line_recv.at[place])
        if self.line:

            @pl.when((place <= here.col) & (here.col < 3))
            def _():
                self.up(step).start()

            @pl.when((place >= here.col) & (here.col > 0))
            def _():
                self.down(step).start()

    def near_step(self, step):
        self.to_across(step).start()
        self.to_along(step).start()
        if self.core:
            self.to_core(0, step).start()

    def plane_step(self, step):
        here, place = self.here, self.order[step]
        arrived(self.block(here.across, place, here.core), self.across_recv.at[place])
        self.corner_one(step).start()
        if self.core:
            self.to_core(1, step).start()
        arrived(self.block(here.along, place, here.core), self.along_recv.at[place])
        self.corner_two(step).start()
        if self.core:
            self.to_core(2, step).start()

    def corner_step(self, step):
        here, place = self.here, self.order[step]
        target = self.block(here.opposite, place, here.core)
        arrived(target.at[self.first], self.one_recv.at[place])
        arrived(target.at[self.second], self.two_recv.at[place])
        if self.core:
            self.to_core(3, step).start()

    def step(self, index):
        if index < self.steps:
            self.line_step(index)
        if self.plane and 0 <= index - 1 < self.steps:
            self.plane_step(index - 1)
        if self.plane and index < self.steps:
            self.near_step(index)
        if self.plane and 0 <= index - 2 < self.steps:
            self.corner_step(index - 2)

    def core_arrived(self, which, step):
        here, place = self.here, self.order[step]
        target = self.block(here.rows[which], place, 1 - here.core)
        arrived(target, self.core_recv.at[which, place])

    def finish(self, arrivals=True):
        here = self.here
        for step in range(self.steps):
            place = self.order[step]
            if self.line:

                @pl.when((place <= here.col) & (here.col < 3))
                def _():
                    self.up(step).wait_send()

                @pl.when((place >= here.col) & (here.col > 0))
                def _():
                    self.down(step).wait_send()

            if self.plane:
                self.to_across(step).wait_send()
                self.to_along(step).wait_send()
                self.corner_one(step).wait_send()
                self.corner_two(step).wait_send()
                for which in range(4 if self.core else 0):
                    self.to_core(which, step).wait_send()
                    if arrivals:
                        self.core_arrived(which, step)


COLLECT_SEMS = (
    [pltpu.SemaphoreType.DMA((4,))] * 4
    + [pltpu.SemaphoreType.DMA((2, 4))] * 4
    + [pltpu.SemaphoreType.DMA((2, 4))] * 2
    + [pltpu.SemaphoreType.DMA((2, 5))]
)


def collect_buffers(rows, width):
    return [
        pltpu.VMEM((4, 4, rows, width), BF16),
        pltpu.VMEM((4, rows // 2, width), BF16),
        pltpu.VMEM((4, rows // 2, width), BF16),
        pltpu.VMEM((4, rows, width), BF16),
        pltpu.VMEM((4, rows, width), BF16),
        pltpu.VMEM((5, rows, width), BF16),
    ]


class Collect:
    def __init__(self, here, buffers, sems):
        self.here = here
        self.mine, self.one, self.two, self.from_across, self.from_along, self.line = buffers
        (
            self.one_send, self.one_recv, self.two_send, self.two_recv,
            self.across_send, self.across_recv, self.along_send, self.along_recv,
            self.up_send, self.down_send, self.line_recv,
        ) = sems
        half = self.mine.shape[2] // 2
        self.halves = (pl.ds(0, half), pl.ds(half, half))

    def give_one(self, place):
        here = self.here
        return remote(
            self.mine.at[3, place, self.halves[0]], self.one.at[place],
            self.one_send.at[place], self.one_recv.at[place], here.at_row(here.across),
        )

    def give_two(self, place):
        here = self.here
        return remote(
            self.mine.at[3, place, self.halves[1]], self.two.at[place],
            self.two_send.at[place], self.two_recv.at[place], here.at_row(here.along),
        )

    def give_across(self, place, half):
        here, part = self.here, self.halves[half]
        return remote(
            self.mine.at[1, place, part], self.from_across.at[place, part],
            self.across_send.at[half, place], self.across_recv.at[half, place], here.at_row(here.across),
        )

    def give_along(self, place, half):
        here, part = self.here, self.halves[half]
        return remote(
            self.mine.at[2, place, part], self.from_along.at[place, part],
            self.along_send.at[half, place], self.along_recv.at[half, place], here.at_row(here.along),
        )

    def give_up(self, place, half):
        here, part = self.here, self.halves[half]
        sems = self.up_send.at[half, place], self.line_recv.at[half, place]
        return remote(
            self.mine.at[0, place, part], self.line.at[place, part], *sems, here.at_col(here.col + 1)
        )

    def give_down(self, place, slot, half):
        here, part = self.here, self.halves[half]
        sems = self.down_send.at[half, place], self.line_recv.at[half, slot]
        return remote(
            self.mine.at[0, place, part], self.line.at[slot, part], *sems, here.at_col(here.col - 1)
        )

    def add_line(self, place, slot, half):
        part = self.halves[half]
        arrived(self.line.at[slot, part], self.line_recv.at[half, slot])
        add_into(self.mine.at[0, place, part], self.line.at[slot, part])

    def start_far(self, place):
        self.give_one(place).start()
        self.give_two(place).start()
        self.give_along(place, 1).start()

    def start_near(self, place):
        self.give_across(place, 0).start()

    def corner_step(self, place):
        self.give_two(place).wait_recv()
        add_into(self.mine.at[1, place, self.halves[1]], self.two.at[place])
        self.give_across(place, 1).start()
        self.give_one(place).wait_recv()
        add_into(self.mine.at[2, place, self.halves[0]], self.one.at[place])
        self.give_along(place, 0).start()

    def plane_step(self, place):
        for half in range(2):
            self.give_across(place, half).wait_recv()
            self.give_along(place, half).wait_recv()
        add_into(self.mine.at[0, place], self.from_across.at[place], self.from_along.at[place])

    def line_step(self, place):
        col = self.here.col
        for half in range(2):

            @pl.when(((place > col) & (col > 0)) | ((place < col) & (col < 3)))
            def _():
                self.add_line(place, place, half)

            @pl.when(place > col)
            def _():
                self.give_up(place, half).start()

            @pl.when(place < col - 1)
            def _():
                self.give_down(place, place, half).start()

            @pl.when(place == col - 1)
            def _():
                self.give_down(place, 4, half).start()

    def own_step(self):
        col = self.here.col
        for half in range(2):

            @pl.when(col > 0)
            def _():
                self.add_line(col, col, half)

            @pl.when(col < 3)
            def _():
                self.add_line(col, 4, half)

    def finish(self):
        col = self.here.col
        for place in range(4):
            self.give_one(place).wait_send()
            self.give_two(place).wait_send()
            for half in range(2):
                self.give_across(place, half).wait_send()
                self.give_along(place, half).wait_send()

                @pl.when(place > col)
                def _():
                    self.give_up(place, half).wait_send()

                @pl.when(place < col)
                def _():
                    self.give_down(place, place, half).wait_send()


def doc_start(places, cuts):
    return jnp.where(places >= cuts[1], cuts[1], jnp.where(places >= cuts[0], cuts[0], 0))


def key_blocks(cuts, first_query, rows, scores_of, block_fn):
    def scan(index, carry):
        start = pl.multiple_of(index * rows, rows)
        free = (start >= doc_start(first_query + rows - 1, cuts)) & (start + rows <= first_query + 1)

        @pl.when(free)
        def _():
            block_fn(start, scores_of(start))

        @pl.when(jnp.logical_not(free))
        def _():
            key_place = start + lax.broadcasted_iota(jnp.int32, (rows, rows), 0)
            place = first_query + lax.broadcasted_iota(jnp.int32, (1, rows), 1)
            allowed = (key_place <= place) & (key_place >= doc_start(place, cuts))
            block_fn(start, jnp.where(allowed, scores_of(start), MASKED))

        return carry

    lax.fori_loop(doc_start(first_query, cuts) // rows, first_query // rows + 1, scan, 0)


def attend_kernel(scale, group_tok, cuts, query, keys, values_t, mixed, total, top, summed, acc):
    rows = query.shape[0]
    side = lax.axis_index("exp") % 2
    first_query = side * group_tok + pl.program_id(0) * rows
    top[...] = jnp.full_like(top, MASKED)
    summed[...] = jnp.zeros_like(summed)
    acc[...] = jnp.zeros_like(acc)
    cut = (cuts[0, 0], cuts[0, 1])

    def scores_of(start):
        return contract_cols(keys[pl.ds(start, rows)], query[...]) * scale

    def block_fn(start, scores):
        old = top[...]
        new = jnp.maximum(old, jnp.max(scores, axis=0, keepdims=True))
        weights = jnp.exp(scores - new)
        decay = jnp.exp(old - new)
        top[...] = new
        summed[...] = summed[...] * decay + jnp.sum(weights, axis=0, keepdims=True)
        acc[...] = acc[...] * decay + matmul(values_t[:, pl.ds(start, rows)], weights.astype(BF16))

    key_blocks(cut, first_query, rows, scores_of, block_fn)
    mixed[...] = (acc[...] / summed[...]).T
    total[...] = top[...] + jnp.log(summed[...])


def attend(query, keys, values, cuts, scale, rows=512):
    group_tok, head_size = query.shape
    whole = lambda shape: pl.BlockSpec(shape, lambda i: (0, 0))
    return pl.pallas_call(
        functools.partial(attend_kernel, scale, group_tok),
        grid=(group_tok // rows,),
        in_specs=[
            pl.BlockSpec(memory_space=pltpu.SMEM),
            pl.BlockSpec((rows, head_size), lambda i: (i, 0)),
            whole(keys.shape),
            whole(values.shape[::-1]),
        ],
        out_specs=[
            pl.BlockSpec((rows, head_size), lambda i: (i, 0)),
            pl.BlockSpec((1, rows), lambda i: (0, i)),
        ],
        out_shape=[
            jax.ShapeDtypeStruct((group_tok, head_size), F32),
            jax.ShapeDtypeStruct((1, group_tok), F32),
        ],
        scratch_shapes=[
            pltpu.VMEM((1, rows), F32),
            pltpu.VMEM((1, rows), F32),
            pltpu.VMEM((head_size, rows), F32),
        ],
        compiler_params=pltpu.CompilerParams(vmem_limit_bytes=40 * 2**20),
        cost_estimate=pl.CostEstimate(
            flops=4 * 7 * 2**20 * head_size, bytes_accessed=2**23, transcendentals=7 * 2**20
        ),
    )(cuts[None], query, keys, values.T)


def attend_back_kernel(
    scale, group_tok, cuts, query, keys, keys_t, values, d_mixed, total, delta,
    d_query, d_keys, d_values, acc,
):
    rows = query.shape[0]
    side = lax.axis_index("exp") % 2
    first_query = side * group_tok + pl.program_id(0) * rows
    cut = (cuts[0, 0], cuts[0, 1])

    @pl.when(pl.program_id(0) == 0)
    def _():
        d_keys[...] = jnp.zeros_like(d_keys)
        d_values[...] = jnp.zeros_like(d_values)

    acc[...] = jnp.zeros_like(acc)

    def scores_of(start):
        return contract_cols(keys[pl.ds(start, rows)], query[...]) * scale

    def block_fn(start, scores):
        part = pl.ds(start, rows)
        weights = jnp.exp(scores - total[...])
        d_weights = contract_cols(values[part], d_mixed[...])
        d_scores = (weights * (d_weights - delta[...])).astype(BF16)
        d_values[part] += matmul(weights.astype(BF16), d_mixed[...])
        d_keys[part] += matmul(d_scores, query[...]) * scale
        acc[...] += matmul(keys_t[:, part], d_scores)

    key_blocks(cut, first_query, rows, scores_of, block_fn)
    d_query[...] = (acc[...] * scale).T


def attend_back(query, keys, values, d_mixed, mixed, total, cuts, scale, rows=512):
    group_tok, head_size = query.shape
    delta = jnp.sum(d_mixed.astype(F32) * mixed, axis=1)[None]
    whole = lambda shape: pl.BlockSpec(shape, lambda i: (0, 0))
    block = pl.BlockSpec((rows, head_size), lambda i: (i, 0))
    line = pl.BlockSpec((1, rows), lambda i: (0, i))
    return pl.pallas_call(
        functools.partial(attend_back_kernel, scale, group_tok),
        grid=(group_tok // rows,),
        in_specs=[
            pl.BlockSpec(memory_space=pltpu.SMEM),
            block,
            whole(keys.shape),
            whole(keys.shape[::-1]),
            whole(keys.shape),
            block,
            line,
            line,
        ],
        out_specs=[block, whole(keys.shape), whole(keys.shape)],
        out_shape=[
            jax.ShapeDtypeStruct((group_tok, head_size), F32),
            jax.ShapeDtypeStruct(keys.shape, F32),
            jax.ShapeDtypeStruct(keys.shape, F32),
        ],
        scratch_shapes=[pltpu.VMEM((head_size, rows), F32)],
        compiler_params=pltpu.CompilerParams(vmem_limit_bytes=48 * 2**20),
        cost_estimate=pl.CostEstimate(
            flops=10 * 7 * 2**20 * head_size, bytes_accessed=2**23, transcendentals=7 * 2**20
        ),
    )(cuts[None], query, keys, keys.T, values, d_mixed, total, delta)


def transposed_product(left, right):
    return jnp.dot(left.T, right, preferred_element_type=F32)


def column_of(line):
    return jnp.broadcast_to(line, (128, 128)).T[:, :1]


def line_of(column):
    return jnp.broadcast_to(column, (128, 128)).T[:1]


def expert_kernel(
    normed, grads_all, mask, gate_half, up_half, down_half,
    gate_other, up_other, down_other, router,
    rows_all, out_parts, total, inner_in, grad_gate, grad_up, grad_down,
    their_gates, their_down,
    gate_w, up_w, down_w, masks, x_buf, d_buf, gates_t, weighteds_t, d_gates, d_ups, weighteds, out_buf,
    inner, sum_buf, sum_down, *rest,
):
    here = Here()
    row, col, core = here.row, here.col, here.core
    rows, width = normed.shape
    half = gate_half.shape[1]
    expert = row * 4 + col
    count = len(SPREAD_SEMS)
    collect = Collect(here, rest[:6], rest[6 : 6 + len(COLLECT_SEMS)])
    rest = rest[6 + len(COLLECT_SEMS) :]
    (
        weight_sem, load_sem, store_sem, tile_sem, give_send, give_recv, their_sem, sum_sem,
        inner_send, inner_recv,
    ) = rest[:10]
    sems = rest[10:]

    def x_block(of_row, place, unused_core):
        return rows_all.at[pl.ds(pl.multiple_of((of_row * 4 + place) * rows, rows), rows)]

    def d_block(of_row, place, unused_core):
        return grads_all.at[pl.ds(pl.multiple_of((of_row * 4 + place) * rows, rows), rows)]

    def m_block(of_row, place, unused_core):
        return masks.at[of_row, place]

    spread_x = Spread(here, normed, x_block, rows, sems[:count], core=False)
    spread_m = Spread(here, mask, m_block, mask.shape[0], sems[count:], core=False)
    order = here.near_first

    own_half = pl.ds(pl.multiple_of(core * half, half), half)
    other_half = pl.ds(pl.multiple_of((1 - core) * half, half), half)
    keeps = [
        pltpu.make_async_copy(source, target, weight_sem.at[index])
        for index, (source, target) in enumerate(
            (
                (normed, x_block(row, col, 0)),
                (mask, m_block(row, col, 0)),
                (gate_half, gate_w.at[:, own_half]),
                (up_half, up_w.at[:, own_half]),
                (down_half, down_w.at[own_half]),
                (gate_other, gate_w.at[:, other_half]),
                (up_other, up_w.at[:, other_half]),
                (down_other, down_w.at[other_half]),
            )
        )
    ]
    greet(here.group_peers() + [here.other_core()])
    spread_x.step(0)
    spread_m.step(0)
    for keep in keeps:
        keep.start()

    turns = (3, 2, 1, 0)

    def loads(step):
        return [
            pltpu.make_async_copy(
                source(here.rows[which], order[step], 0),
                target.at[pl.ds(position * rows, rows)],
                load_sem.at[position, array],
            )
            for position, which in enumerate(turns)
            for array, (source, target) in enumerate(((x_block, x_buf), (d_block, d_buf)))
        ]

    def stores(step):
        return [
            pltpu.make_async_copy(
                out_buf.at[pl.ds(position * rows, rows)],
                out_parts.at[which, order[step]],
                store_sem.at[position],
            )
            for position, which in enumerate(turns)
        ]

    tile = 256

    def first_products(step):
        place = order[step]
        x = x_buf[...]
        lane = lax.broadcasted_iota(jnp.int32, (x.shape[0], router.shape[0]), 1)
        logits = contract_cols(x, router[...])
        raised = jnp.exp(logits - jnp.max(logits, axis=1, keepdims=True))
        picked = jnp.sum(jnp.where(lane == expert, raised, 0.0), axis=1, keepdims=True)
        routed = jnp.concatenate(
            [column_of(masks[here.rows[which], place, pl.ds(expert, 1)]) for which in turns]
        )
        gate = picked / jnp.sum(raised, axis=1, keepdims=True) * routed
        columns = [
            pl.ds(pl.multiple_of((here.rows[which] * 4 + place) * rows, rows), rows) for which in turns
        ]

        def tile_step(index, inner_sum):
            at = pl.ds(pl.multiple_of(index * tile, tile), tile)
            pre_gate = matmul(x_buf[...], gate_w[:, at])
            pre_up = matmul(x_buf[...], up_w[:, at])
            back = contract_cols(d_buf[...], down_w[at])
            sigmoid_gate = 0.5 * jnp.tanh(0.5 * pre_gate) + 0.5
            silu_gate = pre_gate * sigmoid_gate
            hidden = (silu_gate * pre_up).astype(BF16).astype(F32)
            d_hid = back * gate
            d_gate = (d_hid * pre_up * (sigmoid_gate + silu_gate * (1.0 - sigmoid_gate))).astype(BF16)
            d_up = (d_hid * silu_gate).astype(BF16)
            weight = (hidden * gate).astype(BF16)
            d_gates[:, at] = d_gate
            d_ups[:, at] = d_up
            weighteds[:, at] = weight
            side = index // (half // tile)
            first = pl.multiple_of(index % (half // tile) * tile, tile)
            for values, target in (
                (d_gate, gates_t.at[side, pl.ds(first, tile)]),
                (d_up, gates_t.at[side, pl.ds(first + half, tile)]),
                (weight, weighteds_t.at[at]),
            ):
                turned = values.T
                for position, column in enumerate(columns):
                    target[:, column] = turned[:, position * rows : (position + 1) * rows]
            return inner_sum + jnp.sum(hidden * back, axis=1, keepdims=True)

        start = jnp.zeros((x.shape[0], 1), F32)
        inner_sum = lax.fori_loop(0, gate_w.shape[1] // tile, tile_step, start, unroll=2)
        for position, which in enumerate(turns):
            part = slice(position * rows, (position + 1) * rows)
            inner[here.rows[which], place, 0:1] = line_of(inner_sum[part])

    def second_products(step):
        place = order[step]

        @pl.loop(0, width // tile, unroll=2)
        def _(index):
            at = pl.ds(pl.multiple_of(index * tile, tile), tile)
            out_buf[:, at] = matmul(weighteds[...], down_w[:, at]).astype(BF16)
            d_x = contract_cols(d_gates[...], gate_w[at]) + contract_cols(d_ups[...], up_w[at])
            d_x = d_x.astype(BF16)
            for position, which in enumerate(turns):
                collect.mine[which, place, :, at] = d_x[position * rows : (position + 1) * rows]

    for index in (1, 2):
        spread_x.step(index)
        spread_m.step(index)
    for keep in keeps:
        keep.wait()
    for copy in loads(0):
        copy.start()
    turn_order = (0, 1, 3, 2)
    ends = (col == 0) | (col == 3)

    def from_ends(step):
        @pl.when(ends)
        def _():
            collect.line_step(order[step])

    def from_inside(step):
        @pl.when(jnp.logical_not(ends))
        def _():
            collect.line_step(order[step])

    for turn, step in enumerate(turn_order):
        for copy in loads(step):
            copy.wait()
        first_products(step)
        if turn < 2:
            spread_x.step(turn + 3)
            spread_m.step(turn + 3)
        if turn in (0, 2):
            for copy in loads(turn_order[turn + 1]):
                copy.start()
        if turn > 0:
            for copy in stores(turn_order[turn - 1]):
                copy.wait()
            collect.corner_step(order[turn_order[turn - 1]])
        second_products(step)
        for copy in stores(step):
            copy.start()
        collect.start_far(order[step])
        collect.start_near(order[step])
        if turn == 1:
            spread_x.step(5)
            spread_m.step(5)
            for copy in loads(turn_order[2]):
                copy.start()
        if turn > 0:
            collect.plane_step(order[turn_order[turn - 1]])
        if turn > 1:
            from_ends(turn_order[turn - 1])

    tiles = width // tile

    def tile_at(index):
        return pl.ds(pl.multiple_of(index * tile, tile), tile)

    def acts_of(kind, side):
        if kind == 0:
            return gates_t[side]
        return weighteds_t[pl.ds(pl.multiple_of(side * half, half), half)]

    counts = (2 * half, half)

    def slot_at(kind, slot):
        return pl.ds(pl.multiple_of((2 * kind + slot) * tile, tile), tile)

    def tile_buf(kind, slot):
        return gate_w.at[:, slot_at(kind, slot)]

    def give_buf(kind, slot):
        return up_w.at[pl.ds(0, counts[kind]), slot_at(kind, slot)]

    def their_buf(kind, slot):
        return up_w.at[pl.ds(width // 2, counts[kind]), slot_at(kind, slot)]

    theirs = (their_gates, their_down)

    def tile_load(kind, index, slot):
        source = (rows_all, grads_all)[kind]
        return pltpu.make_async_copy(
            source.at[:, tile_at(index)], tile_buf(kind, slot), tile_sem.at[slot]
        )

    def give(kind, index, slot):
        sems = give_send.at[slot, kind], give_recv.at[kind, index]
        return remote(give_buf(kind, slot), theirs[kind].at[:, tile_at(index)], *sems, here.other_core())

    def their_load(kind, index, slot):
        return pltpu.make_async_copy(
            theirs[kind].at[:, tile_at(index)],
            their_buf(kind, slot),
            their_sem.at[slot, kind],
        )

    def sum_stores(kind, index, slot):
        if kind == 1:
            target = grad_down.at[:, tile_at(index)]
            return [pltpu.make_async_copy(sum_down, target, sum_sem.at[0, 2])]
        return [
            pltpu.make_async_copy(
                sum_buf.at[slot, part], target.at[tile_at(index)], sum_sem.at[slot, part]
            )
            for part, target in enumerate((grad_gate, grad_up))
        ]

    def give_gradients(kind, start, stop):
        tile_load(kind, start, 0).start()

        @pl.loop(start, stop)
        def _(index):
            slot = index % 2

            @pl.when(index + 1 < stop)
            def _():
                tile_load(kind, index + 1, 1 - slot).start()

            tile_load(kind, index, slot).wait()
            product = matmul(acts_of(kind, 1 - core), tile_buf(kind, slot)[...])

            @pl.when(index >= 2)
            def _():
                give(kind, index - 2, slot).wait_send()

            give_buf(kind, slot)[...] = product.astype(BF16)
            give(kind, index, slot).start()

    def keep_gradients(kind, start, stop):
        tile_load(kind, start, 0).start()
        give(kind, start, 0).wait_recv()
        their_load(kind, start, 0).start()

        @pl.loop(start, stop)
        def _(index):
            slot = index % 2

            @pl.when(index + 1 < stop)
            def _():
                tile_load(kind, index + 1, 1 - slot).start()
                give(kind, index + 1, 1 - slot).wait_recv()
                their_load(kind, index + 1, 1 - slot).start()

            tile_load(kind, index, slot).wait()
            product = matmul(acts_of(kind, core), tile_buf(kind, slot)[...])
            their_load(kind, index, slot).wait()
            product = product + their_buf(kind, slot)[...].astype(F32)
            held = 2 - kind

            @pl.when(index >= held)
            def _():
                for copy in sum_stores(kind, index - held, slot):
                    copy.wait()

            if kind == 1:
                sum_down[...] = product.astype(BF16)
            else:
                sum_buf[slot, 0] = product[:half].T.astype(BF16)
                sum_buf[slot, 1] = product[half:].T.astype(BF16)
            for copy in sum_stores(kind, index, slot):
                copy.start()

    def give_inner(index):
        step = index + 1
        to_row, to_col = (row + step // 4) % 4, (col + step) % 4
        return remote(
            inner.at[to_row, to_col],
            inner_in.at[row, col],
            inner_send.at[index],
            inner_recv.at[row, col],
            (to_row, to_col, core),
        )

    for index in range(15):
        give_inner(index).start()
    inner_in[row, col] = inner[row, col]
    give_gradients(0, 0, tiles // 2)
    from_inside(3)
    collect.corner_step(order[2])
    give_gradients(0, tiles // 2, tiles)
    collect.plane_step(order[2])
    from_ends(2)
    give_gradients(1, 0, tiles)
    from_inside(2)
    keep_gradients(0, 0, tiles // 2)
    from_inside(1)
    keep_gradients(0, tiles // 2, tiles)
    keep_gradients(1, 0, tiles)
    collect.own_step()
    total[...] = collect.mine[0, col]

    for index in range(15):
        give_inner(index).wait_send()
        step = index + 1
        from_row, from_col = (row + 4 - step // 4) % 4, (col + 4 - step % 4) % 4
        arrived(inner_in.at[from_row, from_col], inner_recv.at[from_row, from_col])
    for copy in stores(turn_order[3]):
        copy.wait()
    for kind in range(2):
        for slot in range(2):
            give(kind, tiles - 2 + slot, slot).wait_send()
        for slot in range(2 - kind):
            for copy in sum_stores(kind, tiles - 2 + kind + slot, slot):
                copy.wait()
    spread_x.finish()
    spread_m.finish()
    collect.finish()


def expert_stage(normed, grads_all, mask, halves, others, router, collective_id):
    rows, width = normed.shape
    half = halves[0].shape[1]
    tokens = 16 * rows
    tile = 256
    vmem = pl.BlockSpec(memory_space=pltpu.VMEM)
    hbm = pl.BlockSpec(memory_space=pl.ANY)
    dma = pltpu.SemaphoreType.DMA
    blocks = jax.ShapeDtypeStruct((4, 4, rows, width), BF16)
    got = pl.pallas_call(
        expert_kernel,
        in_specs=[hbm] * 9 + [vmem],
        out_specs=[hbm] * 2 + [vmem] * 2 + [hbm] * 5,
        out_shape=[
            jax.ShapeDtypeStruct((tokens, width), BF16),
            blocks,
            jax.ShapeDtypeStruct((rows, width), BF16),
            jax.ShapeDtypeStruct((4, 4, 8, rows), F32),
            jax.ShapeDtypeStruct((width, half), BF16),
            jax.ShapeDtypeStruct((width, half), BF16),
            jax.ShapeDtypeStruct((half, width), BF16),
            jax.ShapeDtypeStruct((2 * half, width), BF16),
            jax.ShapeDtypeStruct((half, width), BF16),
        ],
        scratch_shapes=[
            pltpu.VMEM((width, 2 * half), BF16),
            pltpu.VMEM((width, 2 * half), BF16),
            pltpu.VMEM((2 * half, width), BF16),
            pltpu.VMEM((4, 4) + mask.shape, F32),
            pltpu.VMEM((4 * rows, width), BF16),
            pltpu.VMEM((4 * rows, width), BF16),
            pltpu.VMEM((2, 2 * half, tokens), BF16),
            pltpu.VMEM((2 * half, tokens), BF16),
            pltpu.VMEM((4 * rows, 2 * half), BF16),
            pltpu.VMEM((4 * rows, 2 * half), BF16),
            pltpu.VMEM((4 * rows, 2 * half), BF16),
            pltpu.VMEM((4 * rows, width), BF16),
            pltpu.VMEM((4, 4, 8, rows), F32),
            pltpu.VMEM((2, 2, tile, half), BF16),
            pltpu.VMEM((half, tile), BF16),
        ]
        + collect_buffers(rows, width)
        + COLLECT_SEMS
        + [
            dma((8,)), dma((4, 2)), dma((4,)),
            dma((2,)), dma((2, 2)), dma((2, width // tile)), dma((2, 2)), dma((2, 3)),
            dma((15,)), dma((4, 4)),
        ]
        + SPREAD_SEMS * 2,
        compiler_params=pltpu.CompilerParams(
            collective_id=collective_id, has_side_effects=True, vmem_limit_bytes=61 * 2**20
        ),
        cost_estimate=pl.CostEstimate(
            flops=18 * 2 * tokens * width * half,
            bytes_accessed=2**26,
            transcendentals=2 * tokens * half,
        ),
    )(normed, grads_all, mask, *halves, *others, router.T)
    return got[1], got[2], got[3], got[4:7]


def project_kernel(
    hidden, all_gains, weights, cosine, sine,
    normed_out, weights_out, qkv_out, totals, query, keys, values,
    normed, all_weights, qkv, out_sem,
    heads, stat, scale_q, scale_k, kept_sem, kept_kv_sem,
    stat_send, stat_recv, head_send, head_recv, pair_send, pair_recv, *sems,
):
    here = Here()
    row, col, core = here.row, here.col, here.core
    count = len(SPREAD_SEMS)
    rows, width = hidden.shape
    depth = weights.shape[0]
    part = depth // 2

    def weight_block(of_row, unused_place, of_core):
        return all_weights.at[pl.ds(pl.multiple_of(of_row * depth + of_core * part, part), part)]

    def normed_block(unused_row, place, unused_core):
        return normed.at[pl.ds(pl.multiple_of(place * rows, rows), rows)]

    own_weight = weights.at[pl.ds(pl.multiple_of(core * part, part), part)]
    spread_w = Spread(here, own_weight, weight_block, part, sems[:count], line=False)
    spread_n = Spread(
        here, normed_block(row, col, core), normed_block, rows, sems[count:], plane=False
    )
    greet(here.plane_peers() + here.line_peers() + [here.other_core()])
    spread_w.step(0)
    keep = pltpu.make_async_copy(own_weight, weight_block(row, 0, core), kept_sem)
    keep.start()

    values_in = hidden[...].astype(F32)
    scale_one = lax.rsqrt(jnp.mean(values_in * values_in, axis=1, keepdims=True) + EPSILON)
    own_rows = pl.ds(pl.multiple_of(col * rows, rows), rows)
    normed[own_rows] = (values_in * scale_one * all_gains[0:1]).astype(BF16)
    spread_n.step(0)
    spread_w.step(1)
    spread_n.step(1)
    spread_w.step(2)
    spread_n.step(2)
    spread_n.step(3)
    keep.wait()
    for which in range(4):
        spread_w.core_arrived(which, 0)
    puts = [
        pltpu.make_async_copy(source, target, out_sem.at[index])
        for index, (source, target) in enumerate(
            ((normed, normed_out), (all_weights, weights_out), (qkv, qkv_out))
        )
    ]
    puts[0].start()
    puts[1].start()
    columns = 256

    @pl.loop(0, qkv.shape[1] // columns)
    def _(index):
        at = pl.ds(pl.multiple_of(index * columns, columns), columns)
        qkv[:, at] = matmul(normed[...], all_weights[:, at])

    puts[2].start()

    plane = qkv.shape[1] // (3 * HD)
    for kind in range(2):
        square = jnp.zeros((qkv.shape[0], HD), F32)
        for head in range(plane):
            start = (head * 3 + kind) * HD
            raw = qkv[:, start : start + HD]
            square = square + raw * raw
        stat[col, kind : kind + 1] = jnp.sum(square.T, axis=0, keepdims=True)

    def give_stat(step):
        peer = here.line_peers()[step]
        return remote(stat.at[col], stat.at[col], stat_send.at[step], stat_recv.at[col], peer)

    for step in range(3):
        give_stat(step).start()
    for step in range(3):
        place = (col + step + 1) % 4
        arrived(stat.at[place], stat_recv.at[place])
    total = stat[0] + stat[1] + stat[2] + stat[3]
    totals[...] = total
    for kind, target in enumerate((scale_q, scale_k)):
        line = lax.rsqrt(total[kind : kind + 1] / width + EPSILON)
        target[...] = jnp.broadcast_to(line, (HD, line.shape[1])).T

    chunk = 64

    @pl.loop(0, qkv.shape[0] // chunk)
    def _(index):
        at = pl.ds(pl.multiple_of(index * chunk, chunk), chunk)
        for head in range(plane):
            place = pl.ds(pl.multiple_of((col * plane + head) * HD, HD), HD)
            for kind, scales in enumerate((scale_q, scale_k)):
                raw = qkv[at, pl.ds((head * 3 + kind) * HD, HD)]
                unit = raw * scales[at] * all_gains[kind + 1 : kind + 2, place]
                turned = pltpu.roll(unit, HD // 2, 1)
                heads[head, kind, at] = (unit * cosine[at] + turned * sine[at]).astype(BF16)
            heads[head, 2, at] = qkv[at, pl.ds((head * 3 + 2) * HD, HD)].astype(BF16)

    targets = (query.at[row], keys.at[1, row], values.at[1, row])

    def give_head(step, kind):
        dest = here.rows[step + 1]
        sems = head_send.at[step, kind], head_recv.at[kind, row]
        return remote(heads.at[dest, kind], targets[kind], *sems, here.at_row(dest))

    for kind in (1, 2, 0):
        for step in range(3):
            give_head(step, kind).start()

    def give_pair(source, kind):
        array = (keys, values)[kind]
        sems = pair_send.at[kind, source], pair_recv.at[kind, source]
        return remote(array.at[1, source], array.at[0, source], *sems, here.other_core())

    def keep_pair(source, kind):
        array = (keys, values)[kind]
        return pltpu.make_async_copy(
            array.at[1, source], array.at[0, source], kept_kv_sem.at[kind, source]
        )

    def pair_from(source):
        @pl.when(core == 0)
        def _():
            for kind in range(2):
                give_pair(source, kind).start()
                keep_pair(source, kind).start()

    for kind, array in ((1, keys), (2, values)):
        array[1, row] = heads[row, kind]
    query[row] = heads[row, 0]
    pair_from(row)
    for source in here.rows[1:]:
        arrived(keys.at[1, source], head_recv.at[1, source])
        arrived(values.at[1, source], head_recv.at[2, source])
        pair_from(source)
    for source in here.rows[1:]:
        arrived(query.at[source], head_recv.at[0, source])

    @pl.when(core == 0)
    def _():
        for source in range(4):
            for kind in range(2):
                give_pair(source, kind).wait_send()
                keep_pair(source, kind).wait()

    @pl.when(core == 1)
    def _():
        for source in range(4):
            for kind in range(2):
                give_pair(source, kind).wait_recv()

    for step in range(3):
        give_stat(step).wait_send()
        for kind in range(3):
            give_head(step, kind).wait_send()
    for put in puts:
        put.wait()
    spread_w.finish(arrivals=False)
    spread_n.finish()


def project(hidden, gains, weights, cosine, sine, collective_id):
    rows, width = hidden.shape
    depth, columns = weights.shape
    row_tok = 4 * rows
    plane = columns // (3 * HD)
    vmem = pl.BlockSpec(memory_space=pltpu.VMEM)
    hbm = pl.BlockSpec(memory_space=pl.ANY)
    return pl.pallas_call(
        project_kernel,
        in_specs=[vmem, vmem, hbm, vmem, vmem],
        out_specs=[hbm] * 3 + [vmem] * 4,
        out_shape=[
            jax.ShapeDtypeStruct((row_tok, width), BF16),
            jax.ShapeDtypeStruct((4 * depth, columns), BF16),
            jax.ShapeDtypeStruct((row_tok, columns), F32),
            jax.ShapeDtypeStruct((8, row_tok), F32),
            jax.ShapeDtypeStruct((4, row_tok, HD), BF16),
            jax.ShapeDtypeStruct((2, 4, row_tok, HD), BF16),
            jax.ShapeDtypeStruct((2, 4, row_tok, HD), BF16),
        ],
        scratch_shapes=[
            pltpu.VMEM((row_tok, width), BF16),
            pltpu.VMEM((4 * depth, columns), BF16),
            pltpu.VMEM((row_tok, columns), F32),
            pltpu.SemaphoreType.DMA((3,)),
            pltpu.VMEM((plane, 3, row_tok, HD), BF16),
            pltpu.VMEM((4, 8, row_tok), F32),
            pltpu.VMEM((row_tok, HD), F32),
            pltpu.VMEM((row_tok, HD), F32),
            pltpu.SemaphoreType.DMA,
            pltpu.SemaphoreType.DMA((2, 4)),
            pltpu.SemaphoreType.DMA((3,)),
            pltpu.SemaphoreType.DMA((4,)),
            pltpu.SemaphoreType.DMA((3, 3)),
            pltpu.SemaphoreType.DMA((3, 4)),
            pltpu.SemaphoreType.DMA((2, 4)),
            pltpu.SemaphoreType.DMA((2, 4)),
        ]
        + SPREAD_SEMS * 2,
        compiler_params=pltpu.CompilerParams(
            collective_id=collective_id, has_side_effects=True, vmem_limit_bytes=56 * 2**20
        ),
    )(hidden, gains, weights, cosine, sine)


def attention_kernel(
    scale, cuts, query, keys, values, out_weights, hidden, all_gains,
    mixed, total, whole_out, mixed_rows, middle, normed,
    all_out, put_sem, values_t, top, summed, acc, mixed_low, mixed_tok, kept_sem,
    row_send, row_recv, token_send, token_recv, *sems,
):
    here = Here()
    row, col, core = here.row, here.col, here.core
    rows = hidden.shape[0]
    row_tok = 4 * rows
    group_tok = 4 * row_tok
    side = out_weights.shape[0]

    def out_block(of_row, place, of_core):
        start = pl.multiple_of(place * side + of_core * (side // 2), side // 2)
        return all_out.at[pl.ds(start, side // 2), pl.ds(pl.multiple_of(of_row * side, side), side)]

    own_out = out_weights.at[pl.ds(pl.multiple_of(core * (side // 2), side // 2), side // 2)]
    spread = Spread(here, own_out, out_block, side // 2, sems)
    keep = pltpu.make_async_copy(own_out, out_block(row, col, core), kept_sem)
    keep.start()
    values_t[...] = values[...].T
    greet(here.plane_peers() + here.line_peers() + [here.other_core()])
    spread.step(0)
    cut = (cuts[0, 0], cuts[0, 1])
    last_query = 2 * group_tok - row_tok

    def queries(index):
        at = pl.ds(index * row_tok, row_tok)
        first_query = core * group_tok + index * row_tok
        top[...] = jnp.full_like(top, MASKED)
        summed[...] = jnp.zeros_like(summed)
        acc[...] = jnp.zeros_like(acc)

        def block_fn(part, scores):
            old = top[...]
            new = jnp.maximum(old, jnp.max(scores, axis=0, keepdims=True))
            weight = jnp.exp(scores - new)
            decay = jnp.exp(old - new)
            top[...] = new
            summed[...] = summed[...] * decay + jnp.sum(weight, axis=0, keepdims=True)
            acc[...] = acc[...] * decay + matmul(values_t[:, part], weight.astype(BF16))

        def scan(block, carry):
            first_key = block * row_tok
            part = pl.ds(pl.multiple_of(first_key, row_tok), row_tok)
            masked = (block == 0) | (first_key == first_query) | (first_query == last_query)

            @pl.when(jnp.logical_not(masked))
            def _():
                block_fn(part, contract_cols(keys[part], query[at]) * scale)

            @pl.when(masked)
            def _():
                key_place = first_key + lax.broadcasted_iota(jnp.int32, (row_tok, row_tok), 0)
                place = first_query + lax.broadcasted_iota(jnp.int32, (1, row_tok), 1)
                allowed = (key_place <= place) & (key_place >= doc_start(place, cut))
                scores = contract_cols(keys[part], query[at]) * scale
                block_fn(part, jnp.where(allowed, scores, MASKED))

            return carry

        lax.fori_loop(0, core * 4 + index + 1, scan, 0)
        got = (acc[...] / summed[...]).T
        mixed[at] = got
        mixed_low[index] = got.astype(BF16)
        total[:, at] = top[...] + jnp.log(summed[...])

        @pl.when(row != index)
        def _():
            give_row(index).start()

        @pl.when(row == index)
        def _():
            mixed_rows[row] = mixed_low[index]

    def give_row(index):
        sems_of = row_send.at[index], row_recv.at[row]
        return remote(mixed_low.at[index], mixed_rows.at[row], *sems_of, here.at_row(index))

    def give_token(step):
        place = (col + step) % 4
        part = pl.ds(pl.multiple_of(place * rows, rows), rows)
        sems_of = token_send.at[step], token_recv.at[col]
        return remote(mixed_rows.at[:, part], mixed_tok.at[col], *sems_of, here.at_col(place))

    for index in range(4):
        queries(index)
        spread.step(index + 1)
    for source in here.rows[1:]:
        arrived(mixed_rows.at[source], row_recv.at[source])
    for step in range(1, 4):
        give_token(step).start()
    mixed_tok[col] = mixed_rows[:, pl.ds(pl.multiple_of(col * rows, rows), rows)]
    spread.step(5)
    keep.wait()
    spread.finish()
    put = pltpu.make_async_copy(all_out, whole_out, put_sem)
    put.start()
    for step in range(1, 4):
        place = (col + 4 - step) % 4
        arrived(mixed_tok.at[place], token_recv.at[place])
    own = jnp.concatenate([mixed_tok[place, head] for place in range(4) for head in range(4)], axis=1)
    tile = 512

    @pl.loop(0, all_out.shape[1] // tile)
    def _(index):
        at = pl.ds(pl.multiple_of(index * tile, tile), tile)
        middle[:, at] = hidden[:, at].astype(F32) + matmul(own, all_out[:, at])

    values_in = middle[...]
    root = lax.rsqrt(jnp.mean(values_in * values_in, axis=1, keepdims=True) + EPSILON)
    normed[...] = (values_in * root * all_gains[3:4]).astype(BF16)
    put.wait()
    for index in range(4):

        @pl.when(row != index)
        def _():
            give_row(index).wait_send()

    for step in range(1, 4):
        give_token(step).wait_send()


def attention_stage(query, keys, values, cuts, out_weights, hidden, gains, scale, collective_id):
    rows, width = hidden.shape
    row_tok, group_tok = 4 * rows, 16 * rows
    vmem, hbm = pl.BlockSpec(memory_space=pltpu.VMEM), pl.BlockSpec(memory_space=pl.ANY)
    dma = pltpu.SemaphoreType.DMA
    return pl.pallas_call(
        functools.partial(attention_kernel, scale),
        in_specs=[pl.BlockSpec(memory_space=pltpu.SMEM)] + [vmem] * 3 + [hbm] + [vmem] * 2,
        out_specs=[vmem] * 2 + [hbm] + [vmem] * 3,
        out_shape=[
            jax.ShapeDtypeStruct((group_tok, HD), F32),
            jax.ShapeDtypeStruct((1, group_tok), F32),
            jax.ShapeDtypeStruct((width, width), BF16),
            jax.ShapeDtypeStruct((4, row_tok, HD), BF16),
            jax.ShapeDtypeStruct((rows, width), F32),
            jax.ShapeDtypeStruct((rows, width), BF16),
        ],
        scratch_shapes=[
            pltpu.VMEM((width, width), BF16),
            dma,
            pltpu.VMEM((HD, 2 * group_tok), BF16),
            pltpu.VMEM((1, row_tok), F32),
            pltpu.VMEM((1, row_tok), F32),
            pltpu.VMEM((HD, row_tok), F32),
            pltpu.VMEM((4, row_tok, HD), BF16),
            pltpu.VMEM((4, 4, rows, HD), BF16),
            dma, dma((4,)), dma((4,)), dma((4,)), dma((4,)),
        ]
        + SPREAD_SEMS,
        compiler_params=pltpu.CompilerParams(
            collective_id=collective_id, has_side_effects=True, vmem_limit_bytes=40 * 2**20
        ),
    )(cuts, query, keys, values, out_weights, hidden, gains)


class PairSum:
    def __init__(self, here, values, out, held, got, send, recv):
        self.here, self.values, self.out, self.held, self.got = here, values, out, held, got
        self.send, self.recv = send, recv
        col, half = here.col, values.shape[1] // 2
        self.own = pl.ds(pl.multiple_of(here.core * half, half), half)
        self.others = pl.ds(pl.multiple_of((1 - here.core) * half, half), half)
        self.peers = [
            here.at_row(here.across),
            here.at_row(here.along),
            here.at_col(col + 1 - 2 * (col % 2)),
            here.at_col((col + 2) % 4),
        ]

    def copy(self, step):
        here, sems = self.here, (self.send.at[step], self.recv.at[step])
        if step == 0:
            return remote(self.values.at[:, self.others], self.got.at[0], *sems, here.other_core())
        if step == 5:
            return remote(self.held.at[4], self.out.at[:, self.own], *sems, here.other_core())
        return remote(self.held.at[step - 1], self.got.at[step], *sems, self.peers[step - 1])

    def begin(self):
        self.copy(0).start()

    def step(self, index):
        if index == 5:
            arrived(self.out.at[:, self.others], self.recv.at[5])
            return
        self.copy(index).wait_recv()
        before = self.values[:, self.own] if index == 0 else self.held[index - 1]
        self.held[index] = before + self.got[index]
        if index == 4:
            self.out[:, self.own] = self.held[4]
        self.copy(index + 1).start()

    def finish(self):
        for index in range(6):
            self.copy(index).wait_send()


def pair_sum_buffers(rows, width):
    return [
        pltpu.VMEM((5, rows, width // 2), F32),
        pltpu.VMEM((5, rows, width // 2), F32),
        pltpu.SemaphoreType.DMA((6,)),
        pltpu.SemaphoreType.DMA((6,)),
    ]


def back_kernel(
    scale, cuts, d_attn, query, keys, values, mixed, total, out_weights, out_parts, early,
    d_attn_row, d_heads, out_total, early_sum,
    weights, d_mixed_give, d_mixed_row, d_mixed, keys_t, d_keys, d_values, acc, pair_out, pair_in,
    head_give, sum_held, sum_got, sum_send, sum_recv, weight_sem, load_sem,
    near_send, near_recv, head_send, head_recv, back_send, back_recv,
    pair_send, pair_recv, *rest,
):
    here = Here()
    row, col, core = here.row, here.col, here.core
    rows = d_attn.shape[0]
    row_tok = 4 * rows
    group_tok = 4 * row_tok
    plane = 4 * HD
    order = here.near_first[::-1]
    collect = Collect(here, rest[:6], rest[6 : 6 + len(COLLECT_SEMS)])
    sems = rest[6 + len(COLLECT_SEMS) :]

    def row_block(unused_row, place, unused_core):
        return d_attn_row.at[pl.ds(pl.multiple_of(place * rows, rows), rows)]

    spread = Spread(here, row_block(row, col, core), row_block, rows, sems, plane=False)
    pair_sum = PairSum(here, early, early_sum, sum_held, sum_got, sum_send, sum_recv)

    def load(which, place):
        return pltpu.make_async_copy(
            out_parts.at[which, place], collect.mine.at[which, place], load_sem.at[which, place]
        )

    load_weights = pltpu.make_async_copy(out_weights, weights, weight_sem)
    load_weights.start()
    for place in order:
        for which in (3, 2, 1, 0):
            load(which, place).start()
    keys_t[...] = keys[...].T
    d_attn_row[pl.ds(pl.multiple_of(col * rows, rows), rows)] = d_attn[...]
    greet(here.plane_peers() + here.line_peers() + [here.other_core()])

    def give_near(step):
        place = (col + step) % 4
        sems_of = near_send.at[step], near_recv.at[col]
        return remote(d_mixed_give.at[place], d_mixed_row.at[col], *sems_of, here.at_col(place))

    def give_head(step):
        dest = here.rows[step]
        part = pl.ds(pl.multiple_of(dest * HD, HD), HD)
        sems_of = head_send.at[step], head_recv.at[row]
        return remote(d_mixed_row.at[:, :, part], d_mixed.at[row], *sems_of, here.at_row(dest))

    def start(index):
        for which in (3, 2, 1):
            load(which, order[index]).wait()
        collect.start_far(order[index])
        collect.start_near(order[index])

    ends = (col == 0) | (col == 3)

    def from_ends(index):
        @pl.when(ends)
        def _():
            collect.line_step(order[index])

    def from_inside(index):
        @pl.when(jnp.logical_not(ends))
        def _():
            collect.line_step(order[index])

    def plane_part(index):
        load(0, order[index]).wait()
        collect.plane_step(order[index])

    start(0)
    pair_sum.begin()
    load_weights.wait()
    for step in (1, 2, 3, 0):
        place = (col + step) % 4
        part = pl.ds(pl.multiple_of(place * plane, plane), plane)
        product = contract_cols(d_attn[...], weights[part]).astype(BF16)
        if step == 0:
            d_mixed_row[col] = product
        else:
            d_mixed_give[place] = product
            give_near(step).start()
    spread.step(0)
    pair_sum.step(0)
    d_keys[...] = jnp.zeros_like(d_keys)
    d_values[...] = jnp.zeros_like(d_values)
    for step in range(1, 4):
        place = (col + 4 - step) % 4
        arrived(d_mixed_row.at[place], near_recv.at[place])
    for step in range(1, 4):
        give_head(step).start()
    d_mixed[row] = d_mixed_row[:, :, pl.ds(pl.multiple_of(row * HD, HD), HD)]
    collect.corner_step(order[0])
    start(1)
    pair_sum.step(1)
    spread.step(1)
    for source in here.rows[1:]:
        arrived(d_mixed.at[source], head_recv.at[source])

    cut = (cuts[0, 0], cuts[0, 1])
    last_query = 2 * group_tok - row_tok

    def queries(index):
        at = pl.ds(index * row_tok, row_tok)
        first_query = core * group_tok + index * row_tok
        gradient = d_mixed[index].reshape(row_tok, HD)
        delta = jnp.sum((gradient.astype(F32) * mixed[at]).T, axis=0, keepdims=True)
        sums = total[:, at]
        acc[...] = jnp.zeros_like(acc)

        def block_fn(part, scores):
            weight = jnp.exp(scores - sums)
            d_weight = contract_cols(values[part], gradient)
            d_scores = (weight * (d_weight - delta)).astype(BF16)
            d_values[part] += matmul(weight.astype(BF16), gradient)
            d_keys[part] += matmul(d_scores, query[at]) * scale
            acc[...] += matmul(keys_t[:, part], d_scores)

        def scan(block, carry):
            first_key = block * row_tok
            part = pl.ds(pl.multiple_of(first_key, row_tok), row_tok)
            masked = (block == 0) | (first_key == first_query) | (first_query == last_query)

            @pl.when(jnp.logical_not(masked))
            def _():
                block_fn(part, contract_cols(keys[part], query[at]) * scale)

            @pl.when(masked)
            def _():
                key_place = first_key + lax.broadcasted_iota(jnp.int32, (row_tok, row_tok), 0)
                place = first_query + lax.broadcasted_iota(jnp.int32, (1, row_tok), 1)
                allowed = (key_place <= place) & (key_place >= doc_start(place, cut))
                scores = contract_cols(keys[part], query[at]) * scale
                block_fn(part, jnp.where(allowed, scores, MASKED))

            return carry

        lax.fori_loop(0, core * 4 + index + 1, scan, 0)
        head_give[0, index] = (acc[...] * scale).T.astype(BF16)

    queries(0)
    plane_part(0)
    from_ends(0)
    collect.corner_step(order[1])
    start(2)
    spread.step(2)
    queries(1)
    from_inside(0)
    plane_part(1)
    from_ends(1)
    collect.corner_step(order[2])
    start(3)
    pair_sum.step(2)
    queries(2)
    from_inside(1)
    plane_part(2)
    from_ends(2)
    collect.corner_step(order[3])
    spread.step(3)
    queries(3)

    def give_back(step, kind):
        dest = here.rows[step]
        sems_of = back_send.at[step, kind], back_recv.at[kind, row]
        return remote(head_give.at[kind, dest], d_heads.at[row, kind], *sems_of, here.at_row(dest))

    def give_pair(kind):
        sems_of = pair_send.at[kind], pair_recv.at[kind]
        return remote(pair_out.at[kind], pair_in.at[kind], *sems_of, here.other_core())

    for step in range(1, 4):
        give_back(step, 0).start()
    d_heads[row, 0] = head_give[0, row]

    @pl.when(core == 1)
    def _():
        for kind, gradient in enumerate((d_keys, d_values)):
            pair_out[kind] = gradient[pl.ds(0, group_tok)].astype(BF16)
            give_pair(kind).start()
        for kind, gradient in enumerate((d_keys, d_values)):
            for part in range(4):
                at = pl.ds(group_tok + part * row_tok, row_tok)
                head_give[kind + 1, part] = gradient[at].astype(BF16)

    from_inside(2)
    plane_part(3)
    pair_sum.step(3)

    @pl.when(core == 0)
    def _():
        for kind, gradient in enumerate((d_keys, d_values)):
            give_pair(kind).wait_recv()
            for part in range(4):
                at = pl.ds(part * row_tok, row_tok)
                summed = gradient[at] + pair_in[kind, at].astype(F32)
                head_give[kind + 1, part] = summed.astype(BF16)

    for kind in (1, 2):
        for step in range(1, 4):
            give_back(step, kind).start()
        d_heads[row, kind] = head_give[kind, row]
    pair_sum.step(4)
    pair_sum.step(5)
    collect.own_step()
    out_total[...] = collect.mine[0, col]
    for source in here.rows[1:]:
        for kind in range(3):
            arrived(d_heads.at[source, kind], back_recv.at[kind, source])
    for step in range(1, 4):
        give_near(step).wait_send()
        give_head(step).wait_send()
        for kind in range(3):
            give_back(step, kind).wait_send()

    @pl.when(core == 1)
    def _():
        for kind in range(2):
            give_pair(kind).wait_send()

    pair_sum.finish()
    spread.finish()
    collect.finish()


def attend_back_stage(
    d_attn, query, keys, values, mixed, total, cuts, out_weights, out_parts, early, scale, collective_id
):
    rows, width = d_attn.shape
    row_tok, group_tok = 4 * rows, 16 * rows
    vmem, hbm = pl.BlockSpec(memory_space=pltpu.VMEM), pl.BlockSpec(memory_space=pl.ANY)
    dma = pltpu.SemaphoreType.DMA
    return pl.pallas_call(
        functools.partial(back_kernel, scale),
        in_specs=[pl.BlockSpec(memory_space=pltpu.SMEM)] + [vmem] * 6 + [hbm] * 2 + [vmem],
        out_specs=[vmem] * 4,
        out_shape=[
            jax.ShapeDtypeStruct((row_tok, width), BF16),
            jax.ShapeDtypeStruct((4, 3, row_tok, HD), BF16),
            jax.ShapeDtypeStruct((rows, width), BF16),
            jax.ShapeDtypeStruct(early.shape, F32),
        ],
        scratch_shapes=[
            pltpu.VMEM((width, width), BF16),
            pltpu.VMEM((4, rows, 4 * HD), BF16),
            pltpu.VMEM((4, rows, 4 * HD), BF16),
            pltpu.VMEM((4, 4, rows, HD), BF16),
            pltpu.VMEM((HD, 2 * group_tok), BF16),
            pltpu.VMEM((2 * group_tok, HD), F32),
            pltpu.VMEM((2 * group_tok, HD), F32),
            pltpu.VMEM((HD, row_tok), F32),
            pltpu.VMEM((2, group_tok, HD), BF16),
            pltpu.VMEM((2, group_tok, HD), BF16),
            pltpu.VMEM((3, 4, row_tok, HD), BF16),
        ]
        + pair_sum_buffers(*early.shape)
        + [
            dma, dma((4, 4)), dma((4,)), dma((4,)), dma((4,)), dma((4,)),
            dma((4, 3)), dma((3, 4)), dma((2,)), dma((2,)),
        ]
        + collect_buffers(rows, width)
        + COLLECT_SEMS
        + SPREAD_SEMS,
        compiler_params=pltpu.CompilerParams(
            collective_id=collective_id, has_side_effects=True, vmem_limit_bytes=58 * 2**20
        ),
    )(cuts, d_attn, query, keys, values, mixed, total, out_weights, out_parts, early)


def tail_kernel(
    d_heads, qkv, totals, all_gains, cosine, sine, weights_in, normed_in, mixed_rows, d_attn_in,
    hidden,
    grad_hidden, grads, late_sum, last_sum,
    weights, normed, d_attn, in_sem, last, last_got, last_send, last_recv, hop, hop_got, hop_send, hop_recv,
    d_qkv, late, mixed, units, stat, scales, sums, sum_held, sum_got, sum_send, sum_recv,
    stat_send, stat_recv,
    line, line_in, whole, give, other, plane, corner_one, corner_two, from_across, from_along,
    up_send, down_send, line_recv, other_send, other_recv,
    one_send, one_recv, two_send, two_recv, across_send, across_recv, along_send, along_recv,
    back_send, back_recv,
):
    here = Here()
    row, col, core = here.row, here.col, here.core
    rows = hidden.shape[0]
    depth, columns = grads.shape
    part = depth // 2
    first, second = pl.ds(0, part // 2), pl.ds(part // 2, part // 2)
    order = here.near_first[::-1]
    qkv_columns = d_qkv.shape[1]
    tile = 512

    def line_products():
        @pl.loop(0, weights.shape[0] // tile)
        def _(index):
            at = pl.ds(pl.multiple_of(index * tile, tile), tile)
            product = contract_cols(d_qkv[...], weights[at]).astype(BF16)
            line[:, :, at] = product.reshape(4, rows, tile)

    line_halves = (pl.ds(0, rows // 2), pl.ds(rows // 2, rows // 2))

    def give_up(place, half):
        at = line_halves[half]
        sems = up_send.at[half, place], line_recv.at[half, place]
        return remote(line.at[place, at], line_in.at[place, at], *sems, here.at_col(col + 1))

    def give_down(place, slot, half):
        at = line_halves[half]
        sems = down_send.at[half, place], line_recv.at[half, slot]
        return remote(line.at[place, at], line_in.at[slot, at], *sems, here.at_col(col - 1))

    def add_line(place, slot, half):
        at = line_halves[half]
        arrived(line_in.at[slot, at], line_recv.at[half, slot])
        add_into(line.at[place, at], line_in.at[slot, at])

    def line_step(place):
        for half in range(2):

            @pl.when(((place > col) & (col > 0)) | ((place < col) & (col < 3)))
            def _():
                add_line(place, place, half)

            @pl.when(place > col)
            def _():
                give_up(place, half).start()

            @pl.when(place < col - 1)
            def _():
                give_down(place, place, half).start()

            @pl.when(place == col - 1)
            def _():
                give_down(place, 4, half).start()

    def row_product(which):
        of_row = here.rows[which]
        at = pl.ds(pl.multiple_of(of_row * depth, depth), depth)
        whole[:, pl.ds(0, qkv_columns)] = transposed_product(normed[:, at], d_qkv[...]).astype(BF16)
        whole[:, pl.ds(qkv_columns, columns - qkv_columns)] = transposed_product(
            mixed[...], d_attn[:, at]
        ).astype(BF16)
        plane[which] = whole[pl.ds(pl.multiple_of(core * part, part), part)]
        give[which] = whole[pl.ds(pl.multiple_of((1 - core) * part, part), part)]
        to_core(which).start()

    def to_core(which):
        sems = other_send.at[which], other_recv.at[which]
        return remote(give.at[which], other.at[which], *sems, here.other_core())

    def own_sum(which):
        to_core(which).wait_recv()
        add_into(plane.at[which], other.at[which])

    give_one = remote(
        plane.at[3, first], corner_one, one_send, one_recv, here.at_row(here.across)
    )
    give_two = remote(
        plane.at[3, second], corner_two, two_send, two_recv, here.at_row(here.along)
    )

    def give_across(index):
        at = (first, second)[index]
        sems = across_send.at[index], across_recv.at[index]
        return remote(plane.at[1, at], from_across.at[at], *sems, here.at_row(here.across))

    def give_along(index):
        at = (first, second)[index]
        sems = along_send.at[index], along_recv.at[index]
        return remote(plane.at[2, at], from_along.at[at], *sems, here.at_row(here.along))

    pair_sum = PairSum(here, late, late_sum, sum_held, sum_got, sum_send, sum_recv)
    takes = [
        pltpu.make_async_copy(source, target, in_sem.at[index])
        for index, (source, target) in enumerate(
            ((weights_in, weights), (normed_in, normed), (d_attn_in, d_attn))
        )
    ]
    for take in takes:
        take.start()
    near = [(step // 2, step % 2) for step in range(1, 8)]

    def near_device(step):
        which, swap = near[step]
        return (here.rows[which], col, (core + swap) % 2)

    greet([near_device(step) for step in range(7)] + here.line_peers())

    width = hidden.shape[1]
    heads = d_heads.shape[0]
    row_tok = d_qkv.shape[0]
    late[...] = jnp.zeros_like(late)
    for kind in range(2):
        root = lax.rsqrt(totals[kind : kind + 1] / width + EPSILON)
        scales[kind] = jnp.broadcast_to(root, (HD, row_tok)).T
        square = jnp.zeros((row_tok, HD), F32)
        for head in range(heads):
            start = (head * 3 + kind) * HD
            raw = qkv[:, start : start + HD]
            given = d_heads[head, kind].astype(F32)
            unit = given * cosine[...] + pltpu.roll(given * sine[...], HD // 2, 1)
            place = pl.ds(pl.multiple_of((col * heads + head) * HD, HD), HD)
            gains = all_gains[kind + 1 : kind + 2, place]
            gain_sum = jnp.sum(unit * raw * scales[kind], axis=0, keepdims=True)
            late[kind : kind + 1, place] = gain_sum
            weighted = unit * gains
            square = square + weighted * raw
            units[kind, head] = weighted
        stat[col, kind : kind + 1] = jnp.sum(square.T, axis=0, keepdims=True)

    def give_stat(step):
        peer = here.line_peers()[step]
        return remote(stat.at[col], stat.at[col], stat_send.at[step], stat_recv.at[col], peer)

    for step in range(3):
        give_stat(step).start()
    for head in range(heads):
        d_qkv[:, (head * 3 + 2) * HD : (head * 3 + 3) * HD] = d_heads[head, 2]
        mixed[:, head * HD : (head + 1) * HD] = mixed_rows[head]
    for step in range(3):
        place = (col + step + 1) % 4
        arrived(stat.at[place], stat_recv.at[place])
    total = stat[0] + stat[1] + stat[2] + stat[3]
    for kind in range(2):
        sums[...] = jnp.broadcast_to(total[kind : kind + 1] / width, (HD, row_tok)).T
        for head in range(heads):
            start = (head * 3 + kind) * HD
            raw = qkv[:, start : start + HD]
            root = scales[kind]
            d_raw = root * units[kind, head] - raw * (root * root * root) * sums[...]
            d_qkv[:, start : start + HD] = d_raw.astype(BF16)
    ends = (col == 0) | (col == 3)
    pair_sum.begin()
    for take in takes:
        take.wait()
    line_products()

    @pl.when(ends)
    def _():
        for place in order[:3]:
            line_step(place)

    def inner_step(place):
        @pl.when(jnp.logical_not(ends))
        def _():
            line_step(place)

    row_product(3)
    row_product(1)
    pair_sum.step(0)
    inner_step(order[0])
    own_sum(3)
    give_one.start()
    give_two.start()
    row_product(2)
    pair_sum.step(1)
    own_sum(1)
    give_across(0).start()
    own_sum(2)
    give_along(1).start()
    inner_step(order[1])
    row_product(0)
    pair_sum.step(2)
    inner_step(order[2])
    give_two.wait_recv()
    add_into(plane.at[1, second], corner_two)
    give_across(1).start()
    give_one.wait_recv()
    add_into(plane.at[2, first], corner_one)
    give_along(0).start()
    own_sum(0)

    for half in range(2):

        @pl.when(col > 0)
        def _():
            add_line(col, col, half)

        @pl.when(col < 3)
        def _():
            add_line(col, 4, half)

    given = line[col].astype(F32)
    tokens = hidden[...].astype(F32)
    root = lax.rsqrt(jnp.mean(tokens * tokens, axis=1, keepdims=True) + EPSILON)
    part_sum = jnp.sum(given * tokens * root, axis=0, keepdims=True)
    eighth = width // 8
    me = row * 2 + core
    for index in range(8):
        last[index : index + 1] = part_sum[:, index * eighth : (index + 1) * eighth]

    def give_last(step):
        sems = last_send.at[step], last_recv.at[me]
        return remote(last, last_got.at[me], *sems, near_device(step))

    def give_hop(step):
        sems = hop_send.at[step], hop_recv.at[col]
        return remote(hop, hop_got.at[col], *sems, here.line_peers()[step])

    for step in range(7):
        give_last(step).start()
    last_got[me] = last[...]
    weighted = given * all_gains[0:1]
    inner = jnp.mean(weighted * tokens, axis=1, keepdims=True)
    grad_hidden[...] = root * weighted - tokens * (root * root * root) * inner
    pair_sum.step(3)
    for step in range(7):
        which, swap = near[step]
        source = here.rows[which] * 2 + (core + swap) % 2
        arrived(last_got.at[source], last_recv.at[source])
    held = last_got[0]
    for index in range(1, 8):
        held = held + last_got[index]
    hop[...] = held
    hop_got[col] = held
    for step in range(3):
        give_hop(step).start()
    pair_sum.step(4)
    for index in range(2):
        give_across(index).wait_recv()
        give_along(index).wait_recv()
    add_into(plane.at[0], from_across, from_along)
    own_half = pl.ds(pl.multiple_of(core * part, part), part)
    give_back = remote(
        plane.at[0], grads.at[own_half], back_send, back_recv, here.other_core()
    )
    give_back.start()
    grads[own_half] = plane[0]
    other_half = grads.at[pl.ds(pl.multiple_of((1 - core) * part, part), part)]
    pair_sum.step(5)
    for step in range(3):
        place = (col + step + 1) % 4
        arrived(hop_got.at[place], hop_recv.at[place])
    last_sum[...] = hop_got[0] + hop_got[1] + hop_got[2] + hop_got[3]
    arrived(other_half, back_recv)
    for step in range(7):
        give_last(step).wait_send()
    for step in range(3):
        give_hop(step).wait_send()
    pair_sum.finish()
    for step in range(3):
        give_stat(step).wait_send()
    give_back.wait_send()
    give_one.wait_send()
    give_two.wait_send()
    for index in range(2):
        give_across(index).wait_send()
        give_along(index).wait_send()
    for which in range(4):
        to_core(which).wait_send()
    for place in order:
        for half in range(2):

            @pl.when(place > col)
            def _():
                give_up(place, half).wait_send()

            @pl.when(place < col)
            def _():
                give_down(place, place, half).wait_send()


def tail_stage(
    d_heads, qkv, totals, gains, cosine, sine, weights, normed, mixed_rows, d_attn, hidden, collective_id
):
    row_tok, qkv_columns = qkv.shape
    rows, width = hidden.shape
    depth = width // 4
    out_columns = width // 4
    columns = qkv_columns + out_columns
    part = depth // 2
    heads = d_heads.shape[0]
    vmem, hbm = pl.BlockSpec(memory_space=pltpu.VMEM), pl.BlockSpec(memory_space=pl.ANY)
    dma = pltpu.SemaphoreType.DMA
    eighth = (8, width // 8)
    one, four = pltpu.SemaphoreType.DMA, pltpu.SemaphoreType.DMA((4,))
    two = pltpu.SemaphoreType.DMA((2,))
    three = pltpu.SemaphoreType.DMA((3,))
    return pl.pallas_call(
        tail_kernel,
        in_specs=[vmem] * 6 + [hbm] * 2 + [vmem, hbm, vmem],
        out_specs=[vmem] * 4,
        out_shape=[
            jax.ShapeDtypeStruct((rows, width), F32),
            jax.ShapeDtypeStruct((depth, columns), BF16),
            jax.ShapeDtypeStruct((8, width), F32),
            jax.ShapeDtypeStruct(eighth, F32),
        ],
        scratch_shapes=[
            pltpu.VMEM(weights.shape, BF16),
            pltpu.VMEM(normed.shape, BF16),
            pltpu.VMEM(d_attn.shape, BF16),
            dma((3,)),
            pltpu.VMEM(eighth, F32),
            pltpu.VMEM((8,) + eighth, F32),
            dma((7,)),
            dma((8,)),
            pltpu.VMEM(eighth, F32),
            pltpu.VMEM((4,) + eighth, F32),
            dma((3,)),
            dma((4,)),
            pltpu.VMEM((row_tok, qkv_columns), BF16),
            pltpu.VMEM((8, width), F32),
            pltpu.VMEM((row_tok, heads * HD), BF16),
            pltpu.VMEM((2, heads, row_tok, HD), F32),
            pltpu.VMEM((4, 8, row_tok), F32),
            pltpu.VMEM((2, row_tok, HD), F32),
            pltpu.VMEM((row_tok, HD), F32),
        ]
        + pair_sum_buffers(8, width)
        + [
            three, four,
            pltpu.VMEM((4, rows, width), BF16),
            pltpu.VMEM((5, rows, width), BF16),
            pltpu.VMEM((depth, columns), BF16),
            pltpu.VMEM((4, part, columns), BF16),
            pltpu.VMEM((4, part, columns), BF16),
            pltpu.VMEM((4, part, columns), BF16),
            pltpu.VMEM((part // 2, columns), BF16),
            pltpu.VMEM((part // 2, columns), BF16),
            pltpu.VMEM((part, columns), BF16),
            pltpu.VMEM((part, columns), BF16),
            dma((2, 4)), dma((2, 4)), dma((2, 5)), four, four,
            one, one, one, one, two, two, two, two,
            one, one,
        ],
        compiler_params=pltpu.CompilerParams(
            collective_id=collective_id, has_side_effects=True, vmem_limit_bytes=58 * 2**20
        ),
    )(
        d_heads, qkv, totals, gains, cosine, sine, weights, normed, mixed_rows, d_attn, hidden
    )


def expert_rows(rows, grads, gate, gate_w, up_w, down_w):
    pre_gate = matmul(rows, gate_w)
    pre_up = matmul(rows, up_w)
    back = contract_cols(grads, down_w)
    sigmoid_gate = jax.nn.sigmoid(pre_gate)
    silu_gate = pre_gate * sigmoid_gate
    hidden = (silu_gate * pre_up).astype(BF16)
    inner = jnp.sum(hidden.astype(F32) * back, axis=-1)
    weighted = (hidden.astype(F32) * gate).astype(BF16)
    d_hid = back * gate
    d_pregate = (d_hid * pre_up * (sigmoid_gate + silu_gate * (1.0 - sigmoid_gate))).astype(BF16)
    d_preup = (d_hid * silu_gate).astype(BF16)
    outputs = matmul(weighted, down_w).astype(BF16)
    d_rows = (contract_cols(d_pregate, gate_w) + contract_cols(d_preup, up_w)).astype(BF16)
    return (
        outputs,
        d_rows,
        inner,
        contract_rows(rows, d_pregate),
        contract_rows(rows, d_preup),
        contract_rows(weighted, grads),
    )


def experts(normed, grads, dense_gates, gate_w, up_w, down_w):
    rows_dev, width = normed.shape
    devices = math.prod(lax.axis_size(axis) for axis in ALL)
    expert_count = dense_gates.shape[1]
    expert = lax.axis_index(ALL) // 2
    parts = max(1, lax.axis_size("exp") // 2)
    step = rows_dev // parts

    def one_part(sums, piece):
        rows, grad_rows, gates = piece
        rows_all = lax.all_gather(rows, ALL, axis=0, tiled=True)
        grads_all = lax.all_gather(grad_rows, ALL, axis=0, tiled=True)
        gates_all = lax.all_gather(gates, ALL, axis=0, tiled=True)
        gate = lax.dynamic_slice_in_dim(gates_all, expert, 1, 1)
        got = expert_rows(rows_all, grads_all, gate, gate_w, up_w, down_w)
        outputs = lax.psum_scatter(got[0], ALL, scatter_dimension=0, tiled=True)
        d_rows = lax.psum_scatter(got[1], ALL, scatter_dimension=0, tiled=True)
        inner = lax.all_to_all(
            got[2].reshape(devices, step), ALL, split_axis=0, concat_axis=0, tiled=True
        )
        inner = inner.reshape(expert_count, 2, step).sum(axis=1).T
        sums = got[3:] if sums is None else tuple(a + b for a, b in zip(sums, got[3:]))
        return sums, (outputs, d_rows, inner)

    if parts == 1:
        sums, (outputs, d_rows, inner) = one_part(None, (normed, grads, dense_gates))
    else:
        start = tuple(jnp.zeros(w.shape, F32) for w in (gate_w, up_w, down_w))
        pieces = tuple(v.reshape(parts, step, -1) for v in (normed, grads, dense_gates))
        sums, got = lax.scan(one_part, start, pieces)
        outputs, d_rows, inner = (v.reshape(rows_dev, -1) for v in got)
    return outputs.astype(F32), d_rows.astype(F32), inner, sums


def experts_here(normed, grads_all, picks, router, halves, others):
    numbers = jnp.arange(router.shape[1], dtype=jnp.int32)
    mask = jnp.any(picks.T[None] == numbers[:, None, None], axis=1).astype(F32)
    out_parts, d_rows, inner, weights = expert_stage(
        normed, grads_all, mask, halves, others, router, 1
    )
    inner = inner[:, :, 0].reshape(router.shape[1], -1).T
    return out_parts, d_rows.astype(F32), inner, weights


def shards(
    hidden_in,
    out_grad,
    attn_gain,
    w_qkv,
    q_gain,
    k_gain,
    w_out,
    moe_gain,
    router,
    w_gate,
    w_up,
    w_down,
    routes,
    doc_cuts,
):
    row_count, col_count = lax.axis_size("row"), lax.axis_size("col")
    tokens = hidden_in[0].astype(F32)
    rows_dev, width = tokens.shape
    heads = w_qkv.shape[1] // (3 * HD)
    plane = heads * HD
    scale = HD ** (-0.5)
    side = lax.axis_index("exp") % 2
    row_tok = rows_dev * col_count
    group_tok = row_tok * row_count
    here = (row_count, col_count, lax.axis_size("exp")) == (4, 4, 2)
    sequence = 0 if here else lax.axis_index("exp") // 2
    cuts = lax.dynamic_index_in_dim(doc_cuts, sequence, 0, keepdims=False)

    if here:
        grads_all = lax.all_gather(out_grad[0], ("row", "col"), axis=0, tiled=True)
        gains = jnp.stack([attn_gain, q_gain, k_gain, moe_gain]).astype(F32)
        other_w = [lax.ppermute(w[0], "exp", [(0, 1), (1, 0)]) for w in (w_gate, w_up, w_down)]

    gain_one = attn_gain.astype(F32)
    scale_one = rms_scale(tokens)
    head_start = lax.axis_index("col") * plane
    gain_q = lax.dynamic_slice_in_dim(q_gain, head_start, plane, 0).astype(F32)
    gain_k = lax.dynamic_slice_in_dim(k_gain, head_start, plane, 0).astype(F32)
    row_places = side * group_tok + lax.axis_index("row") * row_tok + jnp.arange(row_tok, dtype=jnp.int32)
    unused_doc, position = doc_positions(row_places, cuts)
    cosine, sine = rope_tables(position, HD)
    if here:
        signed = jnp.concatenate([-sine[:, : HD // 2], sine[:, HD // 2 :]], axis=1)
        normed_row, qkv_w, qkv, totals, query, keys, values = project(
            hidden_in[0], gains, w_qkv, cosine, signed, 0
        )
        total_q, total_k = totals[0], totals[1]
        query = query.reshape(group_tok, HD)
        key_all, value_all = keys.reshape(-1, HD), values.reshape(-1, HD)
    else:
        normed_one = (tokens * scale_one * gain_one).astype(BF16)
        normed_row = lax.all_gather(normed_one, "col", axis=0, tiled=True)
        qkv_w = lax.all_gather(w_qkv, "row", axis=0, tiled=True)
        out_w = lax.all_gather(
            lax.all_gather(w_out, "row", axis=1, tiled=True), "col", axis=0, tiled=True
        )
        qkv = matmul(normed_row, qkv_w)
    qkv = qkv.reshape(row_tok, heads, 3, HD)
    query_raw, key_raw, value_raw = qkv[:, :, 0], qkv[:, :, 1], qkv[:, :, 2]
    if not here:
        total_q, total_k = lax.psum(
            (jnp.sum(query_raw * query_raw, axis=(1, 2)), jnp.sum(key_raw * key_raw, axis=(1, 2))),
            "col",
        )
    scale_q = lax.rsqrt(total_q / width + EPSILON)[:, None, None]
    scale_k = lax.rsqrt(total_k / width + EPSILON)[:, None, None]
    gain_q, gain_k = gain_q.reshape(heads, HD), gain_k.reshape(heads, HD)
    cosine, sine = cosine[:, None, :], sine[:, None, :]
    if not here:
        query = rotate(query_raw * scale_q * gain_q, cosine, sine).astype(BF16)
        key = rotate(key_raw * scale_k * gain_k, cosine, sine).astype(BF16)
        moved = rows_to_heads(jnp.concatenate([query, key, value_raw.astype(BF16)], axis=-1))
        query, own_pair = moved[:, :HD], moved[:, HD:]
        earlier_pair = from_behind(own_pair, "exp", 1)
        lower_pair = jnp.where(side == 0, own_pair, earlier_pair)
        upper_pair = jnp.where(side == 0, jnp.zeros_like(own_pair), own_pair)
        key_value = jnp.concatenate([lower_pair, upper_pair], axis=0)
        key_all, value_all = key_value[:, :HD], key_value[:, HD:]

    if here:
        mixed_wide, total, out_w, mixed_rows, middle, normed_two = attention_stage(
            query, key_all, value_all, doc_cuts, w_out, hidden_in[0], gains, scale, 4
        )
    else:
        mixed_wide, total = attend(query, key_all, value_all, cuts, scale)
        mixed = mixed_wide.astype(BF16)
        middle = tokens + matmul(heads_to_tokens(mixed), out_w)

    gain_two = moe_gain.astype(F32)
    scale_two = rms_scale(middle)
    if not here:
        normed_two = (middle * scale_two * gain_two).astype(BF16)
    gates_all = jax.nn.softmax(matmul(normed_two, router), axis=-1)
    picks = routes[0]
    chosen = jnp.any(
        picks[:, :, None] == jnp.arange(router.shape[1], dtype=jnp.int32)[None, None, :], axis=1
    )
    grad_out = out_grad[0].astype(F32)
    expert_w = (w_gate[0], w_up[0], w_down[0])
    if here:
        out_parts, d_normed_two, inner, weight_grads = experts_here(
            normed_two, grads_all, picks, router, expert_w, other_w
        )
    else:
        dense_gates = jnp.where(chosen, gates_all, 0.0)
        mixture, d_normed_two, inner, weight_grads = experts(
            normed_two, out_grad[0], dense_gates, *expert_w
        )
    dense = jnp.where(chosen, inner, 0.0)
    d_logits = (gates_all * (dense - jnp.sum(gates_all * dense, axis=-1, keepdims=True))).astype(BF16)
    grad_router = contract_rows(d_logits, normed_two)
    d_normed_two = d_normed_two + contract_cols(d_logits, router)
    grad_moe_gain = jnp.sum(d_normed_two * middle * scale_two, axis=0)
    weighted_two = d_normed_two * gain_two
    d_middle = (
        grad_out
        + scale_two * weighted_two
        - middle * scale_two**3 * jnp.mean(weighted_two * middle, axis=-1, keepdims=True)
    )

    d_attn = d_middle.astype(BF16)
    if here:
        early = jnp.concatenate([grad_moe_gain[None], jnp.zeros((7, width), F32), grad_router])
        d_attn_row, d_heads, mixture, early = attend_back_stage(
            d_attn, query, key_all, value_all, mixed_wide, total, doc_cuts, out_w, out_parts, early, scale, 2
        )
        grad_hidden, grads, late, last = tail_stage(
            d_heads, qkv.reshape(row_tok, -1), totals, gains, cosine[:, 0], signed,
            qkv_w, normed_row, mixed_rows, d_attn_row, hidden_in[0], 3,
        )
        grad_hidden = d_middle + grad_hidden
        grad_qkv = grads[:, : 3 * plane].astype(F32)
        grad_w_out = grads[:, 3 * plane :].astype(F32)
        weight_grads = [value.astype(F32) for value in weight_grads]
        final = middle + mixture.astype(F32)
        summed = (last.reshape(-1), late[0], late[1], early[0], early[8:])
    else:
        final = middle + mixture
        mixed_row = heads_to_rows(mixed).reshape(row_tok, plane)
        d_mixed = tokens_to_heads(contract_cols(d_attn, out_w).astype(BF16))
        d_attn_row = lax.all_gather(d_attn, "col", axis=0, tiled=True)
        d_query, acc_key, acc_value = attend_back(
            query, key_all, value_all, d_mixed, mixed_wide, total, cuts, scale
        )
        accumulated = jnp.concatenate([acc_key, acc_value], axis=1)
        lower_acc, upper_acc = accumulated[:group_tok], accumulated[group_tok:]
        kept_acc = jnp.where(side == 0, lower_acc, upper_acc)
        later_acc = from_behind(lower_acc.astype(BF16), "exp", -1).astype(F32)
        summed_pair = kept_acc + jnp.where(side == 0, later_acc, jnp.zeros_like(later_acc))
        d_heads = heads_to_rows(jnp.concatenate([d_query, summed_pair], axis=1).astype(BF16)).astype(F32)
        d_q_unit = rotate_back(d_heads[:, :, :HD], cosine, sine)
        d_k_unit = rotate_back(d_heads[:, :, HD : 2 * HD], cosine, sine)
        d_value = d_heads[:, :, 2 * HD :]
        weighted_q = d_q_unit * gain_q
        weighted_k = d_k_unit * gain_k
        sum_q, sum_k = lax.psum(
            (jnp.sum(weighted_q * query_raw, axis=(1, 2)), jnp.sum(weighted_k * key_raw, axis=(1, 2))),
            "col",
        )
        d_query_raw = scale_q * weighted_q - query_raw * scale_q**3 * (sum_q / width)[:, None, None]
        d_key_raw = scale_k * weighted_k - key_raw * scale_k**3 * (sum_k / width)[:, None, None]
        grad_q_part = jnp.sum(d_q_unit * query_raw * scale_q, axis=0).reshape(plane)
        grad_k_part = jnp.sum(d_k_unit * key_raw * scale_k, axis=0).reshape(plane)
        d_qkv = jnp.concatenate([d_query_raw, d_key_raw, d_value], axis=2).astype(BF16)
        d_qkv = d_qkv.reshape(row_tok, heads * 3 * HD)
        d_normed_one = lax.psum_scatter(
            contract_cols(d_qkv, qkv_w).astype(BF16), "col", scatter_dimension=0, tiled=True
        ).astype(F32)
        grad_qkv = lax.psum_scatter(
            contract_rows(normed_row, d_qkv).astype(BF16), "row", scatter_dimension=0, tiled=True
        )
        grad_w_out = lax.psum_scatter(
            contract_rows(mixed_row, d_attn_row).astype(BF16), "row", scatter_dimension=1, tiled=True
        )
        grad_qkv = lax.psum(grad_qkv, "exp").astype(F32)
        grad_w_out = lax.psum(grad_w_out, "exp").astype(F32)
        grad_attn_gain = jnp.sum(d_normed_one * tokens * scale_one, axis=0)
        weighted_one = d_normed_one * gain_one
        grad_hidden = (
            d_middle
            + scale_one * weighted_one
            - tokens * scale_one**3 * jnp.mean(weighted_one * tokens, axis=-1, keepdims=True)
        )
        empty = jnp.zeros((width,), F32)
        grad_q_full = lax.dynamic_update_slice_in_dim(empty, grad_q_part, head_start, 0)
        grad_k_full = lax.dynamic_update_slice_in_dim(empty, grad_k_part, head_start, 0)
        parts = (grad_attn_gain, grad_q_full, grad_k_full, grad_moe_gain)
        summed = lax.psum(parts + (grad_router,), ALL)
    return (
        final.astype(BF16)[None],
        grad_hidden[None],
        summed[0],
        grad_qkv,
        summed[1],
        summed[2],
        grad_w_out,
        summed[3],
        summed[4].T,
        weight_grads[0][None],
        weight_grads[1][None],
        weight_grads[2][None],
    )


def solution(mesh):
    token_spec = P("exp", ("row", "col"), None)
    expert_spec = P(("row", "col", "exp"), None, None)
    in_specs = (
        token_spec,
        token_spec,
        P(),
        P("row", "col"),
        P(),
        P(),
        P("col", "row"),
        P(),
        P(),
        expert_spec,
        expert_spec,
        expert_spec,
        token_spec,
        P(),
    )
    out_specs = (
        token_spec,
        token_spec,
        P(),
        P("row", "col"),
        P(),
        P(),
        P("col", "row"),
        P(),
        P(),
        expert_spec,
        expert_spec,
        expert_spec,
    )
    return jax.shard_map(shards, mesh=mesh, in_specs=in_specs, out_specs=out_specs, check_vma=False)
```

profile of v0, /device:TPU:0, one launch (start us, length us, event | category | flops | bytes accessed | tf_op | source)
XLA Modules:
  0.0 620.4 jit_solution(10200512889062400666)
XLA Ops:
  8.9 0.7 stack.18
  10.3 0.7 stack.15
  11.0 0.7 stack.16
  11.7 0.7 stack.17
  12.4 0.7 fusion.3
  13.7 1.3 fusion.12
  16.4 1.3 subtract_convert_fusion
  17.7 1.0 fusion.2
  18.8 1.0 pad_maximum_fusion
  20.4 127.0 %shard_map.229 = (bf16[512,2048]{1,0:T(8,128)(2,1)}, bf16[2048,1536]{1,0:T(8,128)(2,1)}, f32[512,1536]{1,0:T(8,128)}, f32[8,512]{1,0:T(8,128)}, bf16[4,512,128]{...) custom-call(bf16[128,2048]{1,0:T(8,128)(2,1)} %bitcast.48, ...), custom_call_target="tpu_custom_call" | custom-call | tf_op jit(solution)/shard_map/pallas_call | solution.py:1237
  147.5 1.2 copy-done.1
  148.8 1.2 copy-done.2
  150.0 1.0 copy-done.4
  151.0 58.2 %shard_map.230 = (f32[2048,128]{1,0:T(8,128)S(1)}, f32[1,2048]{1,0:T(1,128)S(1)}, bf16[2048,2048]{1,0:T(8,128)(2,1)}, bf16[4,512,128]{2,1,0:T(8,128)(2,1)S(1)}, ...) custom-call(s32[1,2]{1,0:T(1,128)S(1)} %copy-done.10, bf16[2048,128]{1,0:T(8,128)(2,1)S(1)} %bitcast.56, ...), custom_call_target="tpu_custom_call" | custom-call | tf_op jit(solution)/shard_map/pallas_call | solution.py:1404
  209.2 1.0 copy-done.5
  210.2 0.8 copy-done.7
  212.4 192.6 %shard_map.231 = (bf16[2048,2048]{1,0:T(8,128)(2,1)}, bf16[4,4,128,2048]{3,2,1,0:T(8,128)(2,1)}, bf16[128,2048]{1,0:T(8,128)(2,1)}, f32[4,4,8,128]{3,2,1,0:T(8,1...) custom-call(bf16[128,2048]{1,0:T(8,128)(2,1)} %copy-done.3, ...), custom_call_target="tpu_custom_call" | custom-call | flops 77309411328 | bytes 67108864 | tf_op jit(solution)/shard_map/pallas_call | solution.py:1017
  405.0 0.9 slice.34
  405.9 1.2 fusion.14
  407.2 1.6 multiply_reduce_fusion
  408.8 0.8 pad_maximum_fusion.2.early
  409.5 1.2 fusion.9
  410.8 115.4 %shard_map.232 = (bf16[512,2048]{1,0:T(8,128)(2,1)}, bf16[4,3,512,128]{3,2,1,0:T(8,128)(2,1)}, bf16[128,2048]{1,0:T(8,128)(2,1)}, f32[24,2048]{1,0:T(8,128)}) custom-call(s32[1,2]{1,0:T(1,128)} %cuts.3, bf16[128,2048]{1,0:T(8,128)(2,1)} %get-tuple-element.68.d_attn, bf16[2048,128]{1,0:T(8,128)(2,1)} %bitcast.55, bf16[4096,128]{1,0:T(8,128)(2,1)} %bitcast.51, ...), custom_call_target="tpu_custom_call" | custom-call | tf_op jit(solution)/shard_map/pallas_call | solution.py:1716
  526.2 67.8 %shard_map.233 = (f32[128,2048]{1,0:T(8,128)}, bf16[512,2048]{1,0:T(8,128)(2,1)}, f32[8,2048]{1,0:T(8,128)}, f32[8,256]{1,0:T(8,128)}) custom-call(bf16[4,3,512,128]{3,2,1,0:T(8,128)(2,1)} %get-tuple-element.51.d_heads, f32[512,1536]{1,0:T(8,128)} %get-tuple-element.52.qkv, f32[8,512]{1,0:T(8,128)} %get-tuple-element.53.totals, ...), custom_call_target="tpu_custom_call" | custom-call | tf_op jit(solution)/shard_map/pallas_call | solution.py:2061
  594.0 3.5 slice_convert_fusion
  597.6 2.3 slice_convert_fusion.1
  601.1 1.5 fusion.11
  603.3 0.9 fusion.1
  604.2 2.5 bitcast_convert_fusion
  606.7 2.6 bitcast_convert_fusion.1
  609.3 2.6 bitcast_convert_fusion.2
  612.0 1.1 add_bitcast_fusion
  (67 shorter events, 7.1 us)
Async XLA Ops:
  7.2 204.9 %all-gather.3.cloned.1.call-start = ((), (), s32[]{:S(2)}) async-start(), calls=%async_computation | async-start | bytes 8912896 | tf_op jit(solution)/shard_map/all_gather | solution.py:2215
  7.9 204.2 %collective-permute-start = (bf16[2048,512]{1,0:T(8,128)(2,1)}, bf16[2048,512]{1,0:T(8,128)(2,1)}, u32[]{:S(2)}, u32[]{:S(2)}) collective-permute-start(bf16[2048,512]{1,0:T(8,128)(2,1)} %bitcast.69), channel_id=1, source_target_pairs={{0,1},{1,0},{2,3},{3,2},{4,5},{5,4},{6,7},{7,6},{8,9},{9,8},{10,11... | collective-permute-start | bytes 6291464 | tf_op jit(solution)/shard_map/ppermute | solution.py:2217
  8.4 203.6 %collective-permute-start.1 = (bf16[2048,512]{1,0:T(8,128)(2,1)}, bf16[2048,512]{1,0:T(8,128)(2,1)}, u32[]{:S(2)}, u32[]{:S(2)}) collective-permute-start(bf16[2048,512]{1,0:T(8,128)(2,1)} %bitcast.71), channel_id=1, source_target_pairs={{0,1},{1,0},{2,3},{3,2},{4,5},{5,4},{6,7},{7,6},{8,9},{9,8},{10,11... | collective-permute-start | bytes 6291464 | tf_op jit(solution)/shard_map/ppermute | solution.py:2217
  8.5 203.6 %collective-permute-start.2 = (bf16[512,2048]{1,0:T(8,128)(2,1)}, bf16[512,2048]{1,0:T(8,128)(2,1)}, u32[]{:S(2)}, u32[]{:S(2)}) collective-permute-start(bf16[512,2048]{1,0:T(8,128)(2,1)} %bitcast.73), channel_id=1, source_target_pairs={{0,1},{1,0},{2,3},{3,2},{4,5},{5,4},{6,7},{7,6},{8,9},{9,8},{10,11... | collective-permute-start | bytes 6291464 | tf_op jit(solution)/shard_map/ppermute | solution.py:2217
  18.7 128.8 %copy-start = (bf16[1,128,2048]{2,1,0:T(8,128)(2,1)S(1)}, bf16[1,128,2048]{2,1,0:T(8,128)(2,1)}, u32[]{:S(2)}) copy-start(bf16[1,128,2048]{2,1,0:T(8,128)(2,1)} %param.14) | copy-start | bytes 1572868
  18.8 128.8 %copy-start.8 = (bf16[512,512]{1,0:T(8,128)(2,1)S(1)}, bf16[512,512]{1,0:T(8,128)(2,1)}, u32[]{:S(2)}) copy-start(bf16[512,512]{1,0:T(8,128)(2,1)} %out_weights.1) | copy-start | bytes 1572868
  18.8 128.8 %copy-start.10 = (s32[1,2]{1,0:T(1,128)S(1)}, s32[1,2]{1,0:T(1,128)}, u32[]{:S(2)}) copy-start(s32[1,2]{1,0:T(1,128)} %cuts.3) | copy-start | bytes 28
  20.4 127.1 %copy-start.6 = (f32[4,2048]{1,0:T(4,128)S(1)}, f32[4,2048]{1,0:T(4,128)}, u32[]{:S(2)}) copy-start(f32[4,2048]{1,0:T(4,128)} %maximum_convert_fusion.all_gains) | copy-start | bytes 98308
  20.4 191.1 %copy-start.18 = (bf16[2048,16]{0,1:T(8,128)(2,1)S(1)}, bf16[2048,16]{0,1:T(8,128)(2,1)}, u32[]{:S(2)}) copy-start(bf16[2048,16]{0,1:T(8,128)(2,1)} %param.22) | copy-start | bytes 196612
  147.5 1.2 copy-start.1
  148.8 1.2 copy-start.2
  150.0 1.0 copy-start.4
  151.0 60.8 %copy-start.21 = (s32[1,128,8]{1,2,0:T(8,128)S(1)}, s32[1,128,8]{1,2,0:T(8,128)}, u32[]{:S(2)}) copy-start(s32[1,128,8]{1,2,0:T(8,128)} %param.26) | copy-start | bytes 12292
  209.2 1.0 copy-start.5
  210.2 0.8 copy-start.7
  211.0 0.6 copy-start.9
  211.6 0.8 copy-start.3
  212.4 194.8 %copy-start.19 = (bf16[2048,16]{0,1:T(8,128)(2,1)S(1)}, bf16[2048,16]{0,1:T(8,128)(2,1)}, u32[]{:S(2)}) copy-start(bf16[2048,16]{0,1:T(8,128)(2,1)} %param.22) | copy-start | bytes 196612
  404.9 4.6 copy-start.14
  404.9 4.6 copy-start.15
  594.0 5.9 copy-start.20
  594.0 8.7 %copy-start.22 = (f32[8,256]{1,0:T(8,128)S(1)}, f32[8,256]{1,0:T(8,128)}, u32[]{:S(2)}) copy-start(f32[8,256]{1,0:T(8,128)} %get-tuple-element.59) | copy-start | bytes 24580
  594.0 9.3 %copy-start.17 = (bf16[128,2048]{1,0:T(8,128)(2,1)S(1)}, bf16[128,2048]{1,0:T(8,128)(2,1)}, u32[]{:S(2)}) copy-start(bf16[128,2048]{1,0:T(8,128)(2,1)} %get-tuple-element.50) | copy-start | bytes 1572868
  597.6 6.6 %copy-start.13 = (bf16[512,2048]{1,0:T(8,128)(2,1)S(1)}, bf16[512,2048]{1,0:T(8,128)(2,1)}, u32[]{:S(2)}) copy-start(bf16[512,2048]{1,0:T(8,128)(2,1)} %get-tuple-element.65) | copy-start | bytes 6291460
  604.2 2.5 copy-start.12
  606.7 2.6 copy-start.11
  609.3 2.6 copy-start.16
Sparse Core Ops, SparseCore 0:
  10.8 137.6 all-gather.2
where the time goes:
time: 629 us; the launch traced here: 620 us
  Pallas kernels  561 us (89%)
  other arithmetic  23.8 us (4%)
  between operations  16.1 us (3%)
  local copies, waits for them, and re-layouts  14.6 us (2%)
    pallas_call x1, Pallas kernels, expert_stage(): pl.pallas_call(expert_kernel, in_specs=[hbm] * 9 + [vmem], out_specs=[hbm...  193 us
    pallas_call x1, Pallas kernels, project(): pl.pallas_call(project_kernel, in_specs=[vmem, vmem, hbm, vmem, vmem], ou...  127 us
    pallas_call x1, Pallas kernels, attend_back_stage(): pl.pallas_call(functools.partial(back_kernel, scale), in_specs=[pl.BlockS...  115 us
    pallas_call x1, Pallas kernels, tail_stage(): pl.pallas_call(tail_kernel, in_specs=[vmem] * 6 + [hbm] * 2 + [vmem, hbm,...  67.8 us
    pallas_call x1, Pallas kernels, attention_stage(): pl.pallas_call(functools.partial(attention_kernel, scale), in_specs=[pl.B...  58.2 us
  transfers between devices with their start and end apart: 4, of which 0 were waited for; matrix products, arithmetic and copies ran while one was open for 2% of the time, Pallas kernels for 30%

commit v1 on v0

--- a/solution.py
+++ b/solution.py
@@ -820,6 +820,10 @@
         def _():
             collect.line_step(order[step])
 
+    def start(step):
+        collect.start_far(order[step])
+        collect.start_near(order[step])
+
     for turn, step in enumerate(turn_order):
         for copy in loads(step):
             copy.wait()
@@ -833,21 +837,30 @@
         if turn > 0:
             for copy in stores(turn_order[turn - 1]):
                 copy.wait()
-            collect.corner_step(order[turn_order[turn - 1]])
+        if turn == 2:
+            collect.corner_step(order[1])
+        if turn == 3:
+            collect.corner_step(order[3])
         second_products(step)
         for copy in stores(step):
             copy.start()
-        collect.start_far(order[step])
-        collect.start_near(order[step])
         if turn == 1:
             spread_x.step(5)
             spread_m.step(5)
             for copy in loads(turn_order[2]):
                 copy.start()
-        if turn > 0:
-            collect.plane_step(order[turn_order[turn - 1]])
-        if turn > 1:
-            from_ends(turn_order[turn - 1])
+            start(1)
+            start(0)
+        if turn == 2:
+            start(3)
+            collect.corner_step(order[0])
+            collect.plane_step(order[1])
+            from_ends(1)
+        if turn == 3:
+            start(2)
+            collect.plane_step(order[3])
+            from_ends(3)
+            collect.plane_step(order[0])
 
     tiles = width // tile
 

time: 629 us -> 624 us (level)
    pallas_call x1, Pallas kernels: 115 us -> 107 us  [attend_back_stage(): pl.pallas_call(functools.partial(back_kernel, scale), in_specs=[pl.BlockS...]
where the time goes in v1:
time: 624 us; the launch traced here: 616 us
  Pallas kernels  556 us (89%)
  other arithmetic  23.8 us (4%)
  between operations  16 us (3%)
  local copies, waits for them, and re-layouts  14.6 us (2%)
    pallas_call x1, Pallas kernels, expert_stage(): pl.pallas_call(expert_kernel, in_specs=[hbm] * 9 + [vmem], out_specs=[hbm...  196 us
    pallas_call x1, Pallas kernels, project(): pl.pallas_call(project_kernel, in_specs=[vmem, vmem, hbm, vmem, vmem], ou...  127 us
    pallas_call x1, Pallas kernels, attend_back_stage(): pl.pallas_call(functools.partial(back_kernel, scale), in_specs=[pl.BlockS...  107 us
    pallas_call x1, Pallas kernels, tail_stage(): pl.pallas_call(tail_kernel, in_specs=[vmem] * 6 + [hbm] * 2 + [vmem, hbm,...  68.3 us
    pallas_call x1, Pallas kernels, attention_stage(): pl.pallas_call(functools.partial(attention_kernel, scale), in_specs=[pl.B...  58.2 us
  transfers between devices with their start and end apart: 4, of which 0 were waited for; matrix products, arithmetic and copies ran while one was open for 2% of the time, Pallas kernels for 30%

profile of v1, /device:TPU:0, one launch (start us, length us, event | category | flops | bytes accessed | tf_op | source)
XLA Modules:
  0.0 615.7 jit_solution(7807991369451131242)
XLA Ops:
  8.9 0.7 stack.18
  10.3 0.7 stack.15
  11.0 0.7 stack.16
  11.7 0.7 stack.17
  12.4 0.7 fusion.3
  13.7 1.3 fusion.12
  16.4 1.3 subtract_convert_fusion
  17.7 1.0 fusion.2
  18.8 1.0 pad_maximum_fusion
  20.4 127.0 %shard_map.229 = (bf16[512,2048]{1,0:T(8,128)(2,1)}, bf16[2048,1536]{1,0:T(8,128)(2,1)}, f32[512,1536]{1,0:T(8,128)}, f32[8,512]{1,0:T(8,128)}, bf16[4,512,128]{...) custom-call(bf16[128,2048]{1,0:T(8,128)(2,1)} %bitcast.48, ...), custom_call_target="tpu_custom_call" | custom-call | tf_op jit(solution)/shard_map/pallas_call | solution.py:1250
  147.5 1.2 copy-done.1
  148.8 1.2 copy-done.2
  150.0 1.0 copy-done.4
  151.0 58.2 %shard_map.230 = (f32[2048,128]{1,0:T(8,128)S(1)}, f32[1,2048]{1,0:T(1,128)S(1)}, bf16[2048,2048]{1,0:T(8,128)(2,1)}, bf16[4,512,128]{2,1,0:T(8,128)(2,1)S(1)}, ...) custom-call(s32[1,2]{1,0:T(1,128)S(1)} %copy-done.10, bf16[2048,128]{1,0:T(8,128)(2,1)S(1)} %bitcast.56, ...), custom_call_target="tpu_custom_call" | custom-call | tf_op jit(solution)/shard_map/pallas_call | solution.py:1417
  209.2 1.0 copy-done.5
  210.2 0.8 copy-done.7
  212.4 195.5 %shard_map.231 = (bf16[2048,2048]{1,0:T(8,128)(2,1)}, bf16[4,4,128,2048]{3,2,1,0:T(8,128)(2,1)}, bf16[128,2048]{1,0:T(8,128)(2,1)}, f32[4,4,8,128]{3,2,1,0:T(8,1...) custom-call(bf16[128,2048]{1,0:T(8,128)(2,1)} %copy-done.3, ...), custom_call_target="tpu_custom_call" | custom-call | flops 77309411328 | bytes 67108864 | tf_op jit(solution)/shard_map/pallas_call | solution.py:1030
  407.9 0.9 slice.34
  408.9 1.2 fusion.14
  410.1 1.6 multiply_reduce_fusion
  411.8 0.8 pad_maximum_fusion.2.early
  412.5 1.2 fusion.9
  413.7 107.2 %shard_map.232 = (bf16[512,2048]{1,0:T(8,128)(2,1)}, bf16[4,3,512,128]{3,2,1,0:T(8,128)(2,1)}, bf16[128,2048]{1,0:T(8,128)(2,1)}, f32[24,2048]{1,0:T(8,128)}) custom-call(s32[1,2]{1,0:T(1,128)} %cuts.3, bf16[128,2048]{1,0:T(8,128)(2,1)} %get-tuple-element.68.d_attn, bf16[2048,128]{1,0:T(8,128)(2,1)} %bitcast.55, bf16[4096,128]{1,0:T(8,128)(2,1)} %bitcast.51, ...), custom_call_target="tpu_custom_call" | custom-call | tf_op jit(solution)/shard_map/pallas_call | solution.py:1729
  520.9 68.3 %shard_map.233 = (f32[128,2048]{1,0:T(8,128)}, bf16[512,2048]{1,0:T(8,128)(2,1)}, f32[8,2048]{1,0:T(8,128)}, f32[8,256]{1,0:T(8,128)}) custom-call(bf16[4,3,512,128]{3,2,1,0:T(8,128)(2,1)} %get-tuple-element.51.d_heads, f32[512,1536]{1,0:T(8,128)} %get-tuple-element.52.qkv, f32[8,512]{1,0:T(8,128)} %get-tuple-element.53.totals, ...), custom_call_target="tpu_custom_call" | custom-call | tf_op jit(solution)/shard_map/pallas_call | solution.py:2074
  589.3 3.5 slice_convert_fusion
  592.9 2.3 slice_convert_fusion.1
  596.4 1.5 fusion.11
  598.6 0.9 fusion.1
  599.5 2.5 bitcast_convert_fusion
  602.0 2.6 bitcast_convert_fusion.1
  604.6 2.6 bitcast_convert_fusion.2
  607.3 1.1 add_bitcast_fusion
  (67 shorter events, 7.1 us)
Async XLA Ops:
  7.2 204.9 %all-gather.3.cloned.1.call-start = ((), (), s32[]{:S(2)}) async-start(), calls=%async_computation | async-start | bytes 8912896 | tf_op jit(solution)/shard_map/all_gather | solution.py:2228
  7.9 204.2 %collective-permute-start = (bf16[2048,512]{1,0:T(8,128)(2,1)}, bf16[2048,512]{1,0:T(8,128)(2,1)}, u32[]{:S(2)}, u32[]{:S(2)}) collective-permute-start(bf16[2048,512]{1,0:T(8,128)(2,1)} %bitcast.69), channel_id=1, source_target_pairs={{0,1},{1,0},{2,3},{3,2},{4,5},{5,4},{6,7},{7,6},{8,9},{9,8},{10,11... | collective-permute-start | bytes 6291464 | tf_op jit(solution)/shard_map/ppermute | solution.py:2230
  8.4 203.6 %collective-permute-start.1 = (bf16[2048,512]{1,0:T(8,128)(2,1)}, bf16[2048,512]{1,0:T(8,128)(2,1)}, u32[]{:S(2)}, u32[]{:S(2)}) collective-permute-start(bf16[2048,512]{1,0:T(8,128)(2,1)} %bitcast.71), channel_id=1, source_target_pairs={{0,1},{1,0},{2,3},{3,2},{4,5},{5,4},{6,7},{7,6},{8,9},{9,8},{10,11... | collective-permute-start | bytes 6291464 | tf_op jit(solution)/shard_map/ppermute | solution.py:2230
  8.5 203.6 %collective-permute-start.2 = (bf16[512,2048]{1,0:T(8,128)(2,1)}, bf16[512,2048]{1,0:T(8,128)(2,1)}, u32[]{:S(2)}, u32[]{:S(2)}) collective-permute-start(bf16[512,2048]{1,0:T(8,128)(2,1)} %bitcast.73), channel_id=1, source_target_pairs={{0,1},{1,0},{2,3},{3,2},{4,5},{5,4},{6,7},{7,6},{8,9},{9,8},{10,11... | collective-permute-start | bytes 6291464 | tf_op jit(solution)/shard_map/ppermute | solution.py:2230
  18.7 128.8 %copy-start = (bf16[1,128,2048]{2,1,0:T(8,128)(2,1)S(1)}, bf16[1,128,2048]{2,1,0:T(8,128)(2,1)}, u32[]{:S(2)}) copy-start(bf16[1,128,2048]{2,1,0:T(8,128)(2,1)} %param.14) | copy-start | bytes 1572868
  18.8 128.8 %copy-start.8 = (bf16[512,512]{1,0:T(8,128)(2,1)S(1)}, bf16[512,512]{1,0:T(8,128)(2,1)}, u32[]{:S(2)}) copy-start(bf16[512,512]{1,0:T(8,128)(2,1)} %out_weights.1) | copy-start | bytes 1572868
  18.8 128.8 %copy-start.10 = (s32[1,2]{1,0:T(1,128)S(1)}, s32[1,2]{1,0:T(1,128)}, u32[]{:S(2)}) copy-start(s32[1,2]{1,0:T(1,128)} %cuts.3) | copy-start | bytes 28
  20.4 127.1 %copy-start.6 = (f32[4,2048]{1,0:T(4,128)S(1)}, f32[4,2048]{1,0:T(4,128)}, u32[]{:S(2)}) copy-start(f32[4,2048]{1,0:T(4,128)} %maximum_convert_fusion.all_gains) | copy-start | bytes 98308
  20.4 191.1 %copy-start.18 = (bf16[2048,16]{0,1:T(8,128)(2,1)S(1)}, bf16[2048,16]{0,1:T(8,128)(2,1)}, u32[]{:S(2)}) copy-start(bf16[2048,16]{0,1:T(8,128)(2,1)} %param.22) | copy-start | bytes 196612
  147.5 1.2 copy-start.1
  148.8 1.2 copy-start.2
  150.0 1.0 copy-start.4
  151.0 60.8 %copy-start.21 = (s32[1,128,8]{1,2,0:T(8,128)S(1)}, s32[1,128,8]{1,2,0:T(8,128)}, u32[]{:S(2)}) copy-start(s32[1,128,8]{1,2,0:T(8,128)} %param.26) | copy-start | bytes 12292
  209.2 1.0 copy-start.5
  210.2 0.8 copy-start.7
  211.0 0.6 copy-start.9
  211.6 0.8 copy-start.3
  212.4 197.8 %copy-start.19 = (bf16[2048,16]{0,1:T(8,128)(2,1)S(1)}, bf16[2048,16]{0,1:T(8,128)(2,1)}, u32[]{:S(2)}) copy-start(bf16[2048,16]{0,1:T(8,128)(2,1)} %param.22) | copy-start | bytes 196612
  407.9 4.6 copy-start.14
  407.9 4.6 copy-start.15
  589.3 5.9 copy-start.20
  589.3 8.7 %copy-start.22 = (f32[8,256]{1,0:T(8,128)S(1)}, f32[8,256]{1,0:T(8,128)}, u32[]{:S(2)}) copy-start(f32[8,256]{1,0:T(8,128)} %get-tuple-element.59) | copy-start | bytes 24580
  589.3 9.3 %copy-start.17 = (bf16[128,2048]{1,0:T(8,128)(2,1)S(1)}, bf16[128,2048]{1,0:T(8,128)(2,1)}, u32[]{:S(2)}) copy-start(bf16[128,2048]{1,0:T(8,128)(2,1)} %get-tuple-element.50) | copy-start | bytes 1572868
  592.9 6.6 %copy-start.13 = (bf16[512,2048]{1,0:T(8,128)(2,1)S(1)}, bf16[512,2048]{1,0:T(8,128)(2,1)}, u32[]{:S(2)}) copy-start(bf16[512,2048]{1,0:T(8,128)(2,1)} %get-tuple-element.65) | copy-start | bytes 6291460
  599.5 2.5 copy-start.12
  602.0 2.6 copy-start.11
  604.6 2.6 copy-start.16
Sparse Core Ops, SparseCore 0:
  10.8 137.6 all-gather.2

commit v2 on v1

--- a/solution.py
+++ b/solution.py
@@ -790,10 +790,9 @@
 
     def second_products(step):
         place = order[step]
-
-        @pl.loop(0, width // tile, unroll=2)
-        def _(index):
-            at = pl.ds(pl.multiple_of(index * tile, tile), tile)
+        wide = 512
+        for index in range(width // wide):
+            at = pl.ds(index * wide, wide)
             out_buf[:, at] = matmul(weighteds[...], down_w[:, at]).astype(BF16)
             d_x = contract_cols(d_gates[...], gate_w[at]) + contract_cols(d_ups[...], up_w[at])
             d_x = d_x.astype(BF16)

time: 624 us -> 623 us (level)
  no operation moved by 1% of the time
where the time goes in v2:
time: 623 us; the launch traced here: 615 us
  Pallas kernels  556 us (89%)
  other arithmetic  23.8 us (4%)
  between operations  16 us (3%)
  local copies, waits for them, and re-layouts  14.6 us (2%)
    pallas_call x1, Pallas kernels, expert_stage(): pl.pallas_call(expert_kernel, in_specs=[hbm] * 9 + [vmem], out_specs=[hbm...  195 us
    pallas_call x1, Pallas kernels, project(): pl.pallas_call(project_kernel, in_specs=[vmem, vmem, hbm, vmem, vmem], ou...  127 us
    pallas_call x1, Pallas kernels, attend_back_stage(): pl.pallas_call(functools.partial(back_kernel, scale), in_specs=[pl.BlockS...  106 us
    pallas_call x1, Pallas kernels, tail_stage(): pl.pallas_call(tail_kernel, in_specs=[vmem] * 6 + [hbm] * 2 + [vmem, hbm,...  69.4 us
    pallas_call x1, Pallas kernels, attention_stage(): pl.pallas_call(functools.partial(attention_kernel, scale), in_specs=[pl.B...  58.2 us
  transfers between devices with their start and end apart: 4, of which 0 were waited for; matrix products, arithmetic and copies ran while one was open for 2% of the time, Pallas kernels for 30%

profile of v2, /device:TPU:0, one launch (start us, length us, event | category | flops | bytes accessed | tf_op | source)
XLA Modules:
  0.0 615.4 jit_solution(1859693890801029539)
XLA Ops:
  8.9 0.7 stack.18
  10.3 0.7 stack.15
  11.0 0.7 stack.16
  11.7 0.7 stack.17
  12.4 0.7 fusion.3
  13.7 1.3 fusion.12
  16.4 1.3 subtract_convert_fusion
  17.7 1.0 fusion.2
  18.8 1.0 pad_maximum_fusion
  20.4 127.0 %shard_map.229 = (bf16[512,2048]{1,0:T(8,128)(2,1)}, bf16[2048,1536]{1,0:T(8,128)(2,1)}, f32[512,1536]{1,0:T(8,128)}, f32[8,512]{1,0:T(8,128)}, bf16[4,512,128]{...) custom-call(bf16[128,2048]{1,0:T(8,128)(2,1)} %bitcast.48, ...), custom_call_target="tpu_custom_call" | custom-call | tf_op jit(solution)/shard_map/pallas_call | solution.py:1249
  147.5 1.2 copy-done.1
  148.8 1.2 copy-done.2
  150.0 1.0 copy-done.4
  151.0 58.2 %shard_map.230 = (f32[2048,128]{1,0:T(8,128)S(1)}, f32[1,2048]{1,0:T(1,128)S(1)}, bf16[2048,2048]{1,0:T(8,128)(2,1)}, bf16[4,512,128]{2,1,0:T(8,128)(2,1)S(1)}, ...) custom-call(s32[1,2]{1,0:T(1,128)S(1)} %copy-done.10, bf16[2048,128]{1,0:T(8,128)(2,1)S(1)} %bitcast.56, ...), custom_call_target="tpu_custom_call" | custom-call | tf_op jit(solution)/shard_map/pallas_call | solution.py:1416
  209.2 1.0 copy-done.5
  210.2 0.8 copy-done.7
  212.4 195.4 %shard_map.231 = (bf16[2048,2048]{1,0:T(8,128)(2,1)}, bf16[4,4,128,2048]{3,2,1,0:T(8,128)(2,1)}, bf16[128,2048]{1,0:T(8,128)(2,1)}, f32[4,4,8,128]{3,2,1,0:T(8,1...) custom-call(bf16[128,2048]{1,0:T(8,128)(2,1)} %copy-done.3, ...), custom_call_target="tpu_custom_call" | custom-call | flops 77309411328 | bytes 67108864 | tf_op jit(solution)/shard_map/pallas_call | solution.py:1029
  407.8 0.9 slice.34
  408.8 1.2 fusion.14
  410.0 1.6 multiply_reduce_fusion
  411.6 0.8 pad_maximum_fusion.2.early
  412.4 1.2 fusion.9
  413.6 106.0 %shard_map.232 = (bf16[512,2048]{1,0:T(8,128)(2,1)}, bf16[4,3,512,128]{3,2,1,0:T(8,128)(2,1)}, bf16[128,2048]{1,0:T(8,128)(2,1)}, f32[24,2048]{1,0:T(8,128)}) custom-call(s32[1,2]{1,0:T(1,128)} %cuts.3, bf16[128,2048]{1,0:T(8,128)(2,1)} %get-tuple-element.68.d_attn, bf16[2048,128]{1,0:T(8,128)(2,1)} %bitcast.55, bf16[4096,128]{1,0:T(8,128)(2,1)} %bitcast.51, ...), custom_call_target="tpu_custom_call" | custom-call | tf_op jit(solution)/shard_map/pallas_call | solution.py:1728
  519.6 69.4 %shard_map.233 = (f32[128,2048]{1,0:T(8,128)}, bf16[512,2048]{1,0:T(8,128)(2,1)}, f32[8,2048]{1,0:T(8,128)}, f32[8,256]{1,0:T(8,128)}) custom-call(bf16[4,3,512,128]{3,2,1,0:T(8,128)(2,1)} %get-tuple-element.51.d_heads, f32[512,1536]{1,0:T(8,128)} %get-tuple-element.52.qkv, f32[8,512]{1,0:T(8,128)} %get-tuple-element.53.totals, ...), custom_call_target="tpu_custom_call" | custom-call | tf_op jit(solution)/shard_map/pallas_call | solution.py:2073
  589.0 3.5 slice_convert_fusion
  592.6 2.3 slice_convert_fusion.1
  596.1 1.5 fusion.11
  598.3 0.9 fusion.1
  599.2 2.5 bitcast_convert_fusion
  601.7 2.6 bitcast_convert_fusion.1
  604.3 2.6 bitcast_convert_fusion.2
  607.0 1.1 add_bitcast_fusion
  (67 shorter events, 7.1 us)
Async XLA Ops:
  7.2 204.9 %all-gather.3.cloned.1.call-start = ((), (), s32[]{:S(2)}) async-start(), calls=%async_computation | async-start | bytes 8912896 | tf_op jit(solution)/shard_map/all_gather | solution.py:2227
  7.9 204.2 %collective-permute-start = (bf16[2048,512]{1,0:T(8,128)(2,1)}, bf16[2048,512]{1,0:T(8,128)(2,1)}, u32[]{:S(2)}, u32[]{:S(2)}) collective-permute-start(bf16[2048,512]{1,0:T(8,128)(2,1)} %bitcast.69), channel_id=1, source_target_pairs={{0,1},{1,0},{2,3},{3,2},{4,5},{5,4},{6,7},{7,6},{8,9},{9,8},{10,11... | collective-permute-start | bytes 6291464 | tf_op jit(solution)/shard_map/ppermute | solution.py:2229
  8.4 203.6 %collective-permute-start.1 = (bf16[2048,512]{1,0:T(8,128)(2,1)}, bf16[2048,512]{1,0:T(8,128)(2,1)}, u32[]{:S(2)}, u32[]{:S(2)}) collective-permute-start(bf16[2048,512]{1,0:T(8,128)(2,1)} %bitcast.71), channel_id=1, source_target_pairs={{0,1},{1,0},{2,3},{3,2},{4,5},{5,4},{6,7},{7,6},{8,9},{9,8},{10,11... | collective-permute-start | bytes 6291464 | tf_op jit(solution)/shard_map/ppermute | solution.py:2229
  8.5 203.6 %collective-permute-start.2 = (bf16[512,2048]{1,0:T(8,128)(2,1)}, bf16[512,2048]{1,0:T(8,128)(2,1)}, u32[]{:S(2)}, u32[]{:S(2)}) collective-permute-start(bf16[512,2048]{1,0:T(8,128)(2,1)} %bitcast.73), channel_id=1, source_target_pairs={{0,1},{1,0},{2,3},{3,2},{4,5},{5,4},{6,7},{7,6},{8,9},{9,8},{10,11... | collective-permute-start | bytes 6291464 | tf_op jit(solution)/shard_map/ppermute | solution.py:2229
  18.7 128.8 %copy-start = (bf16[1,128,2048]{2,1,0:T(8,128)(2,1)S(1)}, bf16[1,128,2048]{2,1,0:T(8,128)(2,1)}, u32[]{:S(2)}) copy-start(bf16[1,128,2048]{2,1,0:T(8,128)(2,1)} %param.14) | copy-start | bytes 1572868
  18.8 128.8 %copy-start.8 = (bf16[512,512]{1,0:T(8,128)(2,1)S(1)}, bf16[512,512]{1,0:T(8,128)(2,1)}, u32[]{:S(2)}) copy-start(bf16[512,512]{1,0:T(8,128)(2,1)} %out_weights.1) | copy-start | bytes 1572868
  18.8 128.7 %copy-start.10 = (s32[1,2]{1,0:T(1,128)S(1)}, s32[1,2]{1,0:T(1,128)}, u32[]{:S(2)}) copy-start(s32[1,2]{1,0:T(1,128)} %cuts.3) | copy-start | bytes 28
  20.4 127.1 %copy-start.6 = (f32[4,2048]{1,0:T(4,128)S(1)}, f32[4,2048]{1,0:T(4,128)}, u32[]{:S(2)}) copy-start(f32[4,2048]{1,0:T(4,128)} %maximum_convert_fusion.all_gains) | copy-start | bytes 98308
  20.4 191.1 %copy-start.18 = (bf16[2048,16]{0,1:T(8,128)(2,1)S(1)}, bf16[2048,16]{0,1:T(8,128)(2,1)}, u32[]{:S(2)}) copy-start(bf16[2048,16]{0,1:T(8,128)(2,1)} %param.22) | copy-start | bytes 196612
  147.5 1.2 copy-start.1
  148.8 1.2 copy-start.2
  150.0 1.0 copy-start.4
  151.0 60.8 %copy-start.21 = (s32[1,128,8]{1,2,0:T(8,128)S(1)}, s32[1,128,8]{1,2,0:T(8,128)}, u32[]{:S(2)}) copy-start(s32[1,128,8]{1,2,0:T(8,128)} %param.26) | copy-start | bytes 12292
  209.2 1.0 copy-start.5
  210.2 0.8 copy-start.7
  211.0 0.6 copy-start.9
  211.6 0.8 copy-start.3
  212.4 197.6 %copy-start.19 = (bf16[2048,16]{0,1:T(8,128)(2,1)S(1)}, bf16[2048,16]{0,1:T(8,128)(2,1)}, u32[]{:S(2)}) copy-start(bf16[2048,16]{0,1:T(8,128)(2,1)} %param.22) | copy-start | bytes 196612
  407.8 4.6 copy-start.14
  407.8 4.6 copy-start.15
  589.0 5.9 copy-start.20
  589.0 8.7 %copy-start.22 = (f32[8,256]{1,0:T(8,128)S(1)}, f32[8,256]{1,0:T(8,128)}, u32[]{:S(2)}) copy-start(f32[8,256]{1,0:T(8,128)} %get-tuple-element.59) | copy-start | bytes 24580
  589.0 9.3 %copy-start.17 = (bf16[128,2048]{1,0:T(8,128)(2,1)S(1)}, bf16[128,2048]{1,0:T(8,128)(2,1)}, u32[]{:S(2)}) copy-start(bf16[128,2048]{1,0:T(8,128)(2,1)} %get-tuple-element.50) | copy-start | bytes 1572868
  592.6 6.6 %copy-start.13 = (bf16[512,2048]{1,0:T(8,128)(2,1)S(1)}, bf16[512,2048]{1,0:T(8,128)(2,1)}, u32[]{:S(2)}) copy-start(bf16[512,2048]{1,0:T(8,128)(2,1)} %get-tuple-element.65) | copy-start | bytes 6291460
  599.2 2.5 copy-start.12
  601.7 2.6 copy-start.11
  604.3 2.6 copy-start.16
Sparse Core Ops, SparseCore 0:
  10.8 137.6 all-gather.2

commit v3 on v1

--- a/solution.py
+++ b/solution.py
@@ -1588,11 +1588,11 @@
         give_head(step).start()
     d_mixed[row] = d_mixed_row[:, :, pl.ds(pl.multiple_of(row * HD, HD), HD)]
     collect.corner_step(order[0])
-    start(1)
     pair_sum.step(1)
     spread.step(1)
     for source in here.rows[1:]:
         arrived(d_mixed.at[source], head_recv.at[source])
+    start(1)
 
     cut = (cuts[0, 0], cuts[0, 1])
     last_query = 2 * group_tok - row_tok

time: 624 us -> 625 us (level)
  no operation moved by 1% of the time
where the time goes in v3:
time: 625 us; the launch traced here: 617 us
  Pallas kernels  557 us (89%)
  other arithmetic  23.8 us (4%)
  between operations  16 us (3%)
  local copies, waits for them, and re-layouts  14.6 us (2%)
    pallas_call x1, Pallas kernels, expert_stage(): pl.pallas_call(expert_kernel, in_specs=[hbm] * 9 + [vmem], out_specs=[hbm...  196 us
    pallas_call x1, Pallas kernels, project(): pl.pallas_call(project_kernel, in_specs=[vmem, vmem, hbm, vmem, vmem], ou...  127 us
    pallas_call x1, Pallas kernels, attend_back_stage(): pl.pallas_call(functools.partial(back_kernel, scale), in_specs=[pl.BlockS...  109 us
    pallas_call x1, Pallas kernels, tail_stage(): pl.pallas_call(tail_kernel, in_specs=[vmem] * 6 + [hbm] * 2 + [vmem, hbm,...  68.2 us
    pallas_call x1, Pallas kernels, attention_stage(): pl.pallas_call(functools.partial(attention_kernel, scale), in_specs=[pl.B...  58.2 us
  transfers between devices with their start and end apart: 4, of which 0 were waited for; matrix products, arithmetic and copies ran while one was open for 2% of the time, Pallas kernels for 30%

profile of v3, /device:TPU:0, one launch (start us, length us, event | category | flops | bytes accessed | tf_op | source)
XLA Modules:
  0.0 616.8 jit_solution(3460127224573349106)
XLA Ops:
  8.9 0.7 stack.18
  10.3 0.7 stack.15
  11.0 0.7 stack.16
  11.7 0.7 stack.17
  12.4 0.7 fusion.3
  13.7 1.3 fusion.12
  16.4 1.3 subtract_convert_fusion
  17.7 1.0 fusion.2
  18.8 1.0 pad_maximum_fusion
  20.4 127.0 %shard_map.229 = (bf16[512,2048]{1,0:T(8,128)(2,1)}, bf16[2048,1536]{1,0:T(8,128)(2,1)}, f32[512,1536]{1,0:T(8,128)}, f32[8,512]{1,0:T(8,128)}, bf16[4,512,128]{...) custom-call(bf16[128,2048]{1,0:T(8,128)(2,1)} %bitcast.48, ...), custom_call_target="tpu_custom_call" | custom-call | tf_op jit(solution)/shard_map/pallas_call | solution.py:1250
  147.5 1.2 copy-done.1
  148.8 1.2 copy-done.2
  150.0 1.0 copy-done.4
  151.0 58.2 %shard_map.230 = (f32[2048,128]{1,0:T(8,128)S(1)}, f32[1,2048]{1,0:T(1,128)S(1)}, bf16[2048,2048]{1,0:T(8,128)(2,1)}, bf16[4,512,128]{2,1,0:T(8,128)(2,1)S(1)}, ...) custom-call(s32[1,2]{1,0:T(1,128)S(1)} %copy-done.10, bf16[2048,128]{1,0:T(8,128)(2,1)S(1)} %bitcast.56, ...), custom_call_target="tpu_custom_call" | custom-call | tf_op jit(solution)/shard_map/pallas_call | solution.py:1417
  209.2 1.0 copy-done.5
  210.2 0.8 copy-done.7
  212.4 195.5 %shard_map.231 = (bf16[2048,2048]{1,0:T(8,128)(2,1)}, bf16[4,4,128,2048]{3,2,1,0:T(8,128)(2,1)}, bf16[128,2048]{1,0:T(8,128)(2,1)}, f32[4,4,8,128]{3,2,1,0:T(8,1...) custom-call(bf16[128,2048]{1,0:T(8,128)(2,1)} %copy-done.3, ...), custom_call_target="tpu_custom_call" | custom-call | flops 77309411328 | bytes 67108864 | tf_op jit(solution)/shard_map/pallas_call | solution.py:1030
  407.9 0.9 slice.34
  408.9 1.2 fusion.14
  410.1 1.6 multiply_reduce_fusion
  411.8 0.8 pad_maximum_fusion.2.early
  412.5 1.2 fusion.9
  413.7 108.5 %shard_map.232 = (bf16[512,2048]{1,0:T(8,128)(2,1)}, bf16[4,3,512,128]{3,2,1,0:T(8,128)(2,1)}, bf16[128,2048]{1,0:T(8,128)(2,1)}, f32[24,2048]{1,0:T(8,128)}) custom-call(s32[1,2]{1,0:T(1,128)} %cuts.3, bf16[128,2048]{1,0:T(8,128)(2,1)} %get-tuple-element.68.d_attn, bf16[2048,128]{1,0:T(8,128)(2,1)} %bitcast.55, bf16[4096,128]{1,0:T(8,128)(2,1)} %bitcast.51, ...), custom_call_target="tpu_custom_call" | custom-call | tf_op jit(solution)/shard_map/pallas_call | solution.py:1729
  522.3 68.2 %shard_map.233 = (f32[128,2048]{1,0:T(8,128)}, bf16[512,2048]{1,0:T(8,128)(2,1)}, f32[8,2048]{1,0:T(8,128)}, f32[8,256]{1,0:T(8,128)}) custom-call(bf16[4,3,512,128]{3,2,1,0:T(8,128)(2,1)} %get-tuple-element.51.d_heads, f32[512,1536]{1,0:T(8,128)} %get-tuple-element.52.qkv, f32[8,512]{1,0:T(8,128)} %get-tuple-element.53.totals, ...), custom_call_target="tpu_custom_call" | custom-call | tf_op jit(solution)/shard_map/pallas_call | solution.py:2074
  590.5 3.5 slice_convert_fusion
  594.0 2.3 slice_convert_fusion.1
  597.6 1.5 fusion.11
  599.7 0.9 fusion.1
  600.6 2.5 bitcast_convert_fusion
  603.2 2.6 bitcast_convert_fusion.1
  605.8 2.6 bitcast_convert_fusion.2
  608.4 1.1 add_bitcast_fusion
  (67 shorter events, 7.1 us)
Async XLA Ops:
  7.2 204.9 %all-gather.3.cloned.1.call-start = ((), (), s32[]{:S(2)}) async-start(), calls=%async_computation | async-start | bytes 8912896 | tf_op jit(solution)/shard_map/all_gather | solution.py:2228
  7.9 204.2 %collective-permute-start = (bf16[2048,512]{1,0:T(8,128)(2,1)}, bf16[2048,512]{1,0:T(8,128)(2,1)}, u32[]{:S(2)}, u32[]{:S(2)}) collective-permute-start(bf16[2048,512]{1,0:T(8,128)(2,1)} %bitcast.69), channel_id=1, source_target_pairs={{0,1},{1,0},{2,3},{3,2},{4,5},{5,4},{6,7},{7,6},{8,9},{9,8},{10,11... | collective-permute-start | bytes 6291464 | tf_op jit(solution)/shard_map/ppermute | solution.py:2230
  8.4 203.6 %collective-permute-start.1 = (bf16[2048,512]{1,0:T(8,128)(2,1)}, bf16[2048,512]{1,0:T(8,128)(2,1)}, u32[]{:S(2)}, u32[]{:S(2)}) collective-permute-start(bf16[2048,512]{1,0:T(8,128)(2,1)} %bitcast.71), channel_id=1, source_target_pairs={{0,1},{1,0},{2,3},{3,2},{4,5},{5,4},{6,7},{7,6},{8,9},{9,8},{10,11... | collective-permute-start | bytes 6291464 | tf_op jit(solution)/shard_map/ppermute | solution.py:2230
  8.5 203.6 %collective-permute-start.2 = (bf16[512,2048]{1,0:T(8,128)(2,1)}, bf16[512,2048]{1,0:T(8,128)(2,1)}, u32[]{:S(2)}, u32[]{:S(2)}) collective-permute-start(bf16[512,2048]{1,0:T(8,128)(2,1)} %bitcast.73), channel_id=1, source_target_pairs={{0,1},{1,0},{2,3},{3,2},{4,5},{5,4},{6,7},{7,6},{8,9},{9,8},{10,11... | collective-permute-start | bytes 6291464 | tf_op jit(solution)/shard_map/ppermute | solution.py:2230
  18.7 128.8 %copy-start = (bf16[1,128,2048]{2,1,0:T(8,128)(2,1)S(1)}, bf16[1,128,2048]{2,1,0:T(8,128)(2,1)}, u32[]{:S(2)}) copy-start(bf16[1,128,2048]{2,1,0:T(8,128)(2,1)} %param.14) | copy-start | bytes 1572868
  18.8 128.8 %copy-start.8 = (bf16[512,512]{1,0:T(8,128)(2,1)S(1)}, bf16[512,512]{1,0:T(8,128)(2,1)}, u32[]{:S(2)}) copy-start(bf16[512,512]{1,0:T(8,128)(2,1)} %out_weights.1) | copy-start | bytes 1572868
  18.8 128.8 %copy-start.10 = (s32[1,2]{1,0:T(1,128)S(1)}, s32[1,2]{1,0:T(1,128)}, u32[]{:S(2)}) copy-start(s32[1,2]{1,0:T(1,128)} %cuts.3) | copy-start | bytes 28
  20.4 127.1 %copy-start.6 = (f32[4,2048]{1,0:T(4,128)S(1)}, f32[4,2048]{1,0:T(4,128)}, u32[]{:S(2)}) copy-start(f32[4,2048]{1,0:T(4,128)} %maximum_convert_fusion.all_gains) | copy-start | bytes 98308
  20.4 191.1 %copy-start.18 = (bf16[2048,16]{0,1:T(8,128)(2,1)S(1)}, bf16[2048,16]{0,1:T(8,128)(2,1)}, u32[]{:S(2)}) copy-start(bf16[2048,16]{0,1:T(8,128)(2,1)} %param.22) | copy-start | bytes 196612
  147.5 1.2 copy-start.1
  148.8 1.2 copy-start.2
  150.0 1.0 copy-start.4
  151.0 60.8 %copy-start.21 = (s32[1,128,8]{1,2,0:T(8,128)S(1)}, s32[1,128,8]{1,2,0:T(8,128)}, u32[]{:S(2)}) copy-start(s32[1,128,8]{1,2,0:T(8,128)} %param.26) | copy-start | bytes 12292
  209.2 1.0 copy-start.5
  210.2 0.8 copy-start.7
  211.0 0.6 copy-start.9
  211.6 0.8 copy-start.3
  212.4 197.8 %copy-start.19 = (bf16[2048,16]{0,1:T(8,128)(2,1)S(1)}, bf16[2048,16]{0,1:T(8,128)(2,1)}, u32[]{:S(2)}) copy-start(bf16[2048,16]{0,1:T(8,128)(2,1)} %param.22) | copy-start | bytes 196612
  407.9 4.6 copy-start.14
  407.9 4.6 copy-start.15
  590.5 5.9 copy-start.20
  590.5 8.7 %copy-start.22 = (f32[8,256]{1,0:T(8,128)S(1)}, f32[8,256]{1,0:T(8,128)}, u32[]{:S(2)}) copy-start(f32[8,256]{1,0:T(8,128)} %get-tuple-element.59) | copy-start | bytes 24580
  590.5 9.3 %copy-start.17 = (bf16[128,2048]{1,0:T(8,128)(2,1)S(1)}, bf16[128,2048]{1,0:T(8,128)(2,1)}, u32[]{:S(2)}) copy-start(bf16[128,2048]{1,0:T(8,128)(2,1)} %get-tuple-element.50) | copy-start | bytes 1572868
  594.0 6.6 %copy-start.13 = (bf16[512,2048]{1,0:T(8,128)(2,1)S(1)}, bf16[512,2048]{1,0:T(8,128)(2,1)}, u32[]{:S(2)}) copy-start(bf16[512,2048]{1,0:T(8,128)(2,1)} %get-tuple-element.65) | copy-start | bytes 6291460
  600.6 2.5 copy-start.12
  603.2 2.6 copy-start.11
  605.8 2.6 copy-start.16
Sparse Core Ops, SparseCore 0:
  10.8 137.6 all-gather.2
